TPU v7x, 512 devices: a whole 4x4x16 slice. The times are simulated.
512 devices in a mesh: thread: 64 (over z_lo, x, core), head: 8 (over z_hi, y).
Axes of the slice: x: 4, y: 4, z: 16 (z_hi: 2, z_lo: 8; z = z_hi * 8 + z_lo), core: 2. Of those that a mesh axis runs over, the one named last changes fastest.
Arguments:
- request_id: int32 [64], P('thread'), may hold values from 0 to 31, never falling along the last dimension, each value on 1 to 3 neighbouring positions
- cache_len: int32 [64], P('thread'), may hold values from 1 to 2048, 43690 in all
- query: bfloat16 [64, 64, 64, 128], P('thread', None, 'head'), may hold values from -6 to 6
- new_key: bfloat16 [64, 64, 8, 128], P('thread', None, 'head'), may hold values from -6 to 6
- new_value: bfloat16 [64, 64, 8, 128], P('thread', None, 'head'), may hold values from -8 to 8
- key_cache: bfloat16 [64, 2048, 8, 128], P('thread', None, 'head'), may hold values from -6 to 6
- value_cache: bfloat16 [64, 2048, 8, 128], P('thread', None, 'head'), may hold values from -5 to 5
- out_weight: bfloat16 [8192, 8192], P('head', 'thread'), may hold values from -0.0625 to 0.0625
Outputs:
- projected: bfloat16 [64, 64, 8192], P(None, 'head', 'thread')
Inputs may be any that keep to these rules, and one draw needn't show every extreme that they name: `request_id`: never falling; each request holds 1 to 3 consecutive threads, and some request exactly 3. `cache_len`: some thread has exactly 2048 filled slots.
All inputs are finite; a program needn't handle non-finite values. No bound on the sum of `cache_len` on one device may be relied on, other than what follows from the above.
Results may differ from a plain program's by a relative error of at most 0.019.
Values may be sent and summed in bfloat16 or wider, within the bound.
No kernel may reach another device: no remote copies, remote signals or barrier semaphores. Data moves between devices by JAX's collectives and lax.ppermute only.
A program may use at most 64 MiB of HBM per device.

v0:
```python
import jax
import jax.numpy as jnp
from jax import lax
from jax.sharding import PartitionSpec as P

STEP_TOK = 16
G_MAX = 3


NEGATIVE = -1e30


def from_behind(value, axis, steps):
    count = lax.axis_size(axis)
    first, last = (max(0, -steps), min(count, count - steps))
    return lax.ppermute(value, axis, [(source, source + steps) for source in range(first, last)])


def partial_block(queries, key_rows, value_rows, allowed, factor):
    scores = (
        jnp.einsum("hrd,khd->hrk", queries, key_rows, preferred_element_type=jnp.float32) * factor
    )
    scores = jnp.where(allowed[None], scores, NEGATIVE)
    row_max = jnp.max(scores, axis=-1)
    weights = jnp.where(allowed[None], jnp.exp(scores - row_max[..., None]), 0.0)
    row_total = jnp.sum(weights, axis=-1)
    summed = jnp.einsum(
        "hrk,khd->hrd", weights.astype(jnp.bfloat16), value_rows, preferred_element_type=jnp.float32
    )
    return (row_max, row_total, summed)


def combine_parts(first, second):
    row_max = jnp.maximum(first[0], second[0])
    scale_one = jnp.exp(first[0] - row_max)
    scale_two = jnp.exp(second[0] - row_max)
    row_total = scale_one * first[1] + scale_two * second[1]
    summed = scale_one[..., None] * first[2] + scale_two[..., None] * second[2]
    return (row_max, row_total, summed)


def local_parts(queries, sibling, cache_rows, row_token, factor, is_own):
    key_rows, value_rows, fresh_keys, fresh_values, length = cache_rows
    capacity = key_rows.shape[0]
    new_count = fresh_keys.shape[0]
    row_count = row_token.shape[0]
    positions = jnp.arange(capacity, dtype=jnp.int32)
    cache_ok = jnp.broadcast_to((positions < length)[None, :] & sibling, (row_count, capacity))
    key_token = jnp.arange(new_count, dtype=jnp.int32)
    if is_own:
        new_ok = key_token[None, :] <= row_token[:, None]
    else:
        new_ok = (key_token[None, :] // STEP_TOK < row_token[:, None] // STEP_TOK) & sibling
    cached = partial_block(queries, key_rows, value_rows, cache_ok, factor)
    fresh = partial_block(queries, fresh_keys, fresh_values, new_ok, factor)
    return combine_parts(cached, fresh)


def body(request_id, cache_len, query, new_key, new_value, key_cache, value_cache, out_weight):
    new_count = query.shape[1]
    head_dim = query.shape[3]
    kv_dev = key_cache.shape[2]
    group_size = query.shape[2] // kv_dev
    factor = head_dim ** (-0.5)
    queries = query[0].reshape(new_count, kv_dev, group_size, head_dim).transpose(1, 0, 2, 3)
    queries = queries.reshape(kv_dev, new_count * group_size, head_dim)
    row_token = jnp.arange(new_count * group_size, dtype=jnp.int32) // group_size
    request_tag = request_id + 1
    own_rows = (key_cache[0], value_cache[0], new_key[0], new_value[0], cache_len[0])
    running = local_parts(queries, jnp.array(True), own_rows, row_token, factor, True)
    distances = [step for reach in range(1, G_MAX) for step in (reach, -reach)]
    for offset in distances:
        arrived = from_behind(
            (key_cache, value_cache, new_key, new_value, cache_len, request_tag), "thread", offset
        )
        sibling = arrived[5][0] == request_tag[0]
        near_rows = (arrived[0][0], arrived[1][0], arrived[2][0], arrived[3][0], arrived[4][0])
        running = combine_parts(
            running, local_parts(queries, sibling, near_rows, row_token, factor, False)
        )
    attended = (running[2] / running[1][..., None]).reshape(kv_dev, new_count, group_size, head_dim)
    attended = (
        attended.transpose(1, 0, 2, 3)
        .reshape(1, new_count, kv_dev * group_size * head_dim)
        .astype(jnp.bfloat16)
    )
    partial_terms = jnp.einsum(
        "tnf,fc->tnc",
        lax.all_gather(attended, "thread", axis=0, tiled=True),
        out_weight,
        preferred_element_type=jnp.float32,
    )
    result = lax.psum_scatter(
        partial_terms.astype(jnp.bfloat16), "head", scatter_dimension=1, tiled=True
    )
    return result


def solution(mesh):
    placed = (
        P("thread"),
        P("thread"),
        P("thread", None, "head", None),
        P("thread", None, "head", None),
        P("thread", None, "head", None),
        P("thread", None, "head", None),
        P("thread", None, "head", None),
        P("head", "thread"),
    )
    return jax.shard_map(
        body, mesh=mesh, in_specs=placed, out_specs=P(None, "head", "thread"), check_vma=False
    )
```

profile of v0, /device:TPU:6, one launch (start us, length us, event | category | flops | bytes accessed | tf_op | source)
XLA Modules:
  0.0 410.0 jit_solution(12548791487595620755)
XLA Ops:
  7.2 3.5 collective-permute-start.5
  10.7 2.7 collective-permute-start.1
  13.4 3.5 collective-permute-start.7
  17.0 3.6 collective-permute-start.3
  20.6 3.2 collective-permute-start.13
  25.6 2.0 fusion
  28.8 1.9 collective-permute-start.4
  31.3 3.3 collective-permute-done.4
  34.7 3.6 collective-permute-start.15
  38.9 4.8 %collective-permute-start = (s32[1]{0:T(128)}, s32[1]{0:T(128)}, u32[]{:S(2)}, u32[]{:S(2)}) collective-permute-start(s32[1]{0:T(128)} %param.9), channel_id=1, source_target_pairs={{0,8},{8,16},{16,24},{24,32},{32,40},{40,48},{48,56},{56,64},{64,7... | collective-permute-start | bytes 20 | tf_op jit(solution)/shard_map/ppermute | solution.py:16
  44.8 7.3 %collective-permute-start.9 = (s32[1]{0:T(128)}, s32[1]{0:T(128)}, u32[]{:S(2)}, u32[]{:S(2)}) collective-permute-start(s32[1]{0:T(128)} %add.142), channel_id=1, source_target_pairs={{0,16},{8,24},{16,32},{24,40},{32,48},{40,56},{48,64},{56,72},{64,... | collective-permute-start | bytes 20 | tf_op jit(solution)/shard_map/ppermute | solution.py:16
  52.7 5.6 %collective-permute-start.8 = (s32[1]{0:T(128)}, s32[1]{0:T(128)}, u32[]{:S(2)}, u32[]{:S(2)}) collective-permute-start(s32[1]{0:T(128)} %param.9), channel_id=1, source_target_pairs={{0,16},{8,24},{16,32},{24,40},{32,48},{40,56},{48,64},{56,72},{64,... | collective-permute-start | bytes 20 | tf_op jit(solution)/shard_map/ppermute | solution.py:16
  59.7 6.4 %collective-permute-start.11 = (bf16[1,64,1,128]{3,1,2,0:T(8,128)(2,1)S(1)}, bf16[1,64,1,128]{3,1,2,0:T(8,128)(2,1)S(1)}, u32[]{:S(2)}, u32[]{:S(2)}) collective-permute-start(bf16[1,64,1,128]{3,1,2,0:T(8,128)(2,1)S(1)} %copy-done.3), channel_id=1, source_target_pairs={{0,16},{8,24},{16,32},{24,40},{32,48},{40,56},{48,64},{56,72},{64,... | collective-permute-start | bytes 49160 | tf_op jit(solution)/shard_map/ppermute | solution.py:16
  69.2 5.3 %collective-permute-done.12 = s32[1]{0:T(128)} collective-permute-done((s32[1]{0:T(128)}, s32[1]{0:T(128)}, u32[]{:S(2)}, u32[]{:S(2)}) %collective-permute-start.12) | collective-permute-done | bytes 36 | tf_op jit(solution)/shard_map/ppermute | solution.py:16
  77.0 2.4 collective-permute-start.2
  81.8 3.9 collective-permute-start.14
  89.9 4.8 %collective-permute-start.21 = (bf16[1,64,1,128]{3,1,2,0:T(8,128)(2,1)S(1)}, bf16[1,64,1,128]{3,1,2,0:T(8,128)(2,1)S(1)}, u32[]{:S(2)}, u32[]{:S(2)}) collective-permute-start(bf16[1,64,1,128]{3,1,2,0:T(8,128)(2,1)S(1)} %copy-done.4), channel_id=1, source_target_pairs={{0,16},{8,24},{16,32},{24,40},{32,48},{40,56},{48,64},{56,72},{64,... | collective-permute-start | bytes 49160 | tf_op jit(solution)/shard_map/ppermute | solution.py:16
  104.4 4.1 %collective-permute-start.23 = (bf16[1,64,1,128]{3,1,2,0:T(8,128)(2,1)S(1)}, bf16[1,64,1,128]{3,1,2,0:T(8,128)(2,1)S(1)}, u32[]{:S(2)}, u32[]{:S(2)}) collective-permute-start(bf16[1,64,1,128]{3,1,2,0:T(8,128)(2,1)S(1)} %copy-done.4), channel_id=1, source_target_pairs={{16,0},{24,8},{32,16},{40,24},{48,32},{56,40},{64,48},{72,56},{80,... | collective-permute-start | bytes 49160 | tf_op jit(solution)/shard_map/ppermute | solution.py:16
  113.8 3.1 collective-permute-start.19
  117.3 2.3 collective-permute-start.18
  120.6 8.6 %collective-permute-done.22 = bf16[1,2048,1,128]{3,1,2,0:T(8,128)(2,1)S(1)} collective-permute-done((bf16[1,2048,1,128]{3,1,2,0:T(8,128)(2,1)S(1)}, bf16[1,2048,1,128]{3,1,2,0:T(8,128)(2,1)S(1)}, u32[]{:S(2)}, u32[]{:S(2)}) %collective-permute-start.22) | collective-permute-done | bytes 524320 | tf_op jit(solution)/shard_map/ppermute | solution.py:16
  134.6 142.7 %all-gather.2.cloned.1.call-done = bf16[64,64,1024]{2,1,0:T(8,128)(2,1)} async-done(((bf16[1,64,1024]{2,1,0:T(8,128)(2,1)}), bf16[64,64,1024]{2,1,0:T(8,128)(2,1)}) %all-gather.2.cloned.1.call-update) | async-done | bytes 8388624 | tf_op jit(solution)/shard_map/all_gather | solution.py:89
  277.3 5.7 %convolution_convert_fusion = bf16[64,64,128]{2,1,0:T(8,128)(2,1)S(1)} fusion(bf16[64,64,1024]{2,1,0:T(8,128)(2,1)} %all-gather.2.cloned.1.call-done, bf16[1024,128]{1,0:T(8,128)(2,1)S(1)} %copy-done), kind=kOutput, calls=%fused_computation.35 | convolution fusion | flops 1074266112 | bytes 9699328 | tf_op jit(solution)/shard_map/tnf,fc->tnc/dot_general | solution.py:87
  285.4 116.1 %reduce-scatter.4.cloned.1.call-done = bf16[8,8192]{1,0:T(8,128)(2,1)} async-done(((bf16[64,8192]{1,0:T(8,128)(2,1)}), bf16[8,8192]{1,0:T(8,128)(2,1)}) %reduce-scatter.4.cloned.1.call-update) | async-done | bytes 131088
  (85 shorter events, 42.0 us)
Async XLA Ops:
  6.5 270.7 %all-gather.2.cloned.1.call-start = ((), (), s32[]{:S(2)}) async-start(), calls=%async_computation.1 | async-start | bytes 8519680 | tf_op jit(solution)/shard_map/all_gather | solution.py:89
  7.2 21.5 %collective-permute-start.5 = (s32[1]{0:T(128)}, s32[1]{0:T(128)}, u32[]{:S(2)}, u32[]{:S(2)}) collective-permute-start(s32[1]{0:T(128)} %add.142), channel_id=1, source_target_pairs={{8,0},{16,8},{24,16},{32,24},{40,32},{48,40},{56,48},{64,56},{72,6... | collective-permute-start | bytes 20 | tf_op jit(solution)/shard_map/ppermute | solution.py:16
  10.7 28.1 %collective-permute-start.1 = (s32[1]{0:T(128)}, s32[1]{0:T(128)}, u32[]{:S(2)}, u32[]{:S(2)}) collective-permute-start(s32[1]{0:T(128)} %add.142), channel_id=1, source_target_pairs={{0,8},{8,16},{16,24},{24,32},{32,40},{40,48},{48,56},{56,64},{64,7... | collective-permute-start | bytes 20 | tf_op jit(solution)/shard_map/ppermute | solution.py:16
  13.4 63.6 %collective-permute-start.7 = (bf16[1,64,1,128]{3,1,2,0:T(8,128)(2,1)}, bf16[1,64,1,128]{3,1,2,0:T(8,128)(2,1)S(1)}, u32[]{:S(2)}, u32[]{:S(2)}) collective-permute-start(bf16[1,64,1,128]{3,1,2,0:T(8,128)(2,1)} %param.11), channel_id=1, source_target_pairs={{8,0},{16,8},{24,16},{32,24},{40,32},{48,40},{56,48},{64,56},{72,6... | collective-permute-start | bytes 49160 | tf_op jit(solution)/shard_map/ppermute | solution.py:16
  17.0 62.7 %collective-permute-start.3 = (bf16[1,64,1,128]{3,1,2,0:T(8,128)(2,1)}, bf16[1,64,1,128]{3,1,2,0:T(8,128)(2,1)S(1)}, u32[]{:S(2)}, u32[]{:S(2)}) collective-permute-start(bf16[1,64,1,128]{3,1,2,0:T(8,128)(2,1)} %param.11), channel_id=1, source_target_pairs={{0,8},{8,16},{16,24},{24,32},{32,40},{40,48},{48,56},{56,64},{64,7... | collective-permute-start | bytes 49160 | tf_op jit(solution)/shard_map/ppermute | solution.py:16
  20.6 46.1 %collective-permute-start.13 = (s32[1]{0:T(128)}, s32[1]{0:T(128)}, u32[]{:S(2)}, u32[]{:S(2)}) collective-permute-start(s32[1]{0:T(128)} %add.142), channel_id=1, source_target_pairs={{16,0},{24,8},{32,16},{40,24},{48,32},{56,40},{64,48},{72,56},{80,... | collective-permute-start | bytes 20 | tf_op jit(solution)/shard_map/ppermute | solution.py:16
  34.7 47.1 %collective-permute-start.15 = (bf16[1,64,1,128]{3,1,2,0:T(8,128)(2,1)S(1)}, bf16[1,64,1,128]{3,1,2,0:T(8,128)(2,1)S(1)}, u32[]{:S(2)}, u32[]{:S(2)}) collective-permute-start(bf16[1,64,1,128]{3,1,2,0:T(8,128)(2,1)S(1)} %copy-done.3), channel_id=1, source_target_pairs={{16,0},{24,8},{32,16},{40,24},{48,32},{56,40},{64,48},{72,56},{80,... | collective-permute-start | bytes 49160 | tf_op jit(solution)/shard_map/ppermute | solution.py:16
  44.8 7.9 %collective-permute-start.9 = (s32[1]{0:T(128)}, s32[1]{0:T(128)}, u32[]{:S(2)}, u32[]{:S(2)}) collective-permute-start(s32[1]{0:T(128)} %add.142), channel_id=1, source_target_pairs={{0,16},{8,24},{16,32},{24,40},{32,48},{40,56},{48,64},{56,72},{64,... | collective-permute-start | bytes 20 | tf_op jit(solution)/shard_map/ppermute | solution.py:16
  52.7 7.0 %collective-permute-start.8 = (s32[1]{0:T(128)}, s32[1]{0:T(128)}, u32[]{:S(2)}, u32[]{:S(2)}) collective-permute-start(s32[1]{0:T(128)} %param.9), channel_id=1, source_target_pairs={{0,16},{8,24},{16,32},{24,40},{32,48},{40,56},{48,64},{56,72},{64,... | collective-permute-start | bytes 20 | tf_op jit(solution)/shard_map/ppermute | solution.py:16
  59.7 26.2 %collective-permute-start.11 = (bf16[1,64,1,128]{3,1,2,0:T(8,128)(2,1)S(1)}, bf16[1,64,1,128]{3,1,2,0:T(8,128)(2,1)S(1)}, u32[]{:S(2)}, u32[]{:S(2)}) collective-permute-start(bf16[1,64,1,128]{3,1,2,0:T(8,128)(2,1)S(1)} %copy-done.3), channel_id=1, source_target_pairs={{0,16},{8,24},{16,32},{24,40},{32,48},{40,56},{48,64},{56,72},{64,... | collective-permute-start | bytes 49160 | tf_op jit(solution)/shard_map/ppermute | solution.py:16
  66.7 7.8 %collective-permute-start.12 = (s32[1]{0:T(128)}, s32[1]{0:T(128)}, u32[]{:S(2)}, u32[]{:S(2)}) collective-permute-start(s32[1]{0:T(128)} %param.9), channel_id=1, source_target_pairs={{16,0},{24,8},{32,16},{40,24},{48,32},{56,40},{64,48},{72,56},{80,... | collective-permute-start | bytes 20 | tf_op jit(solution)/shard_map/ppermute | solution.py:16
  74.5 22.1 %collective-permute-start.6 = (bf16[1,2048,1,128]{3,1,2,0:T(8,128)(2,1)S(1)}, bf16[1,2048,1,128]{3,1,2,0:T(8,128)(2,1)S(1)}, u32[]{:S(2)}, u32[]{:S(2)}) collective-permute-start(bf16[1,2048,1,128]{3,1,2,0:T(8,128)(2,1)S(1)} %copy-done.2), channel_id=1, source_target_pairs={{8,0},{16,8},{24,16},{32,24},{40,32},{48,40},{56,48},{64,56},{72,6... | collective-permute-start | bytes 1572872 | tf_op jit(solution)/shard_map/ppermute | solution.py:16
  77.0 12.8 %collective-permute-start.2 = (bf16[1,2048,1,128]{3,1,2,0:T(8,128)(2,1)S(1)}, bf16[1,2048,1,128]{3,1,2,0:T(8,128)(2,1)S(1)}, u32[]{:S(2)}, u32[]{:S(2)}) collective-permute-start(bf16[1,2048,1,128]{3,1,2,0:T(8,128)(2,1)S(1)} %copy-done.2), channel_id=1, source_target_pairs={{0,8},{8,16},{16,24},{24,32},{32,40},{40,48},{48,56},{56,64},{64,7... | collective-permute-start | bytes 1572872 | tf_op jit(solution)/shard_map/ppermute | solution.py:16
  79.7 20.8 %collective-permute-start.10 = (bf16[1,2048,1,128]{3,1,2,0:T(8,128)(2,1)S(1)}, bf16[1,2048,1,128]{3,1,2,0:T(8,128)(2,1)S(1)}, u32[]{:S(2)}, u32[]{:S(2)}) collective-permute-start(bf16[1,2048,1,128]{3,1,2,0:T(8,128)(2,1)S(1)} %copy-done.2), channel_id=1, source_target_pairs={{0,16},{8,24},{16,32},{24,40},{32,48},{40,56},{48,64},{56,72},{64,... | collective-permute-start | bytes 1572872 | tf_op jit(solution)/shard_map/ppermute | solution.py:16
  81.8 22.6 %collective-permute-start.14 = (bf16[1,2048,1,128]{3,1,2,0:T(8,128)(2,1)S(1)}, bf16[1,2048,1,128]{3,1,2,0:T(8,128)(2,1)S(1)}, u32[]{:S(2)}, u32[]{:S(2)}) collective-permute-start(bf16[1,2048,1,128]{3,1,2,0:T(8,128)(2,1)S(1)} %copy-done.2), channel_id=1, source_target_pairs={{16,0},{24,8},{32,16},{40,24},{48,32},{56,40},{64,48},{72,56},{80,... | collective-permute-start | bytes 1572872 | tf_op jit(solution)/shard_map/ppermute | solution.py:16
  86.0 44.5 %collective-permute-start.17 = (bf16[1,64,1,128]{3,1,2,0:T(8,128)(2,1)S(1)}, bf16[1,64,1,128]{3,1,2,0:T(8,128)(2,1)S(1)}, u32[]{:S(2)}, u32[]{:S(2)}) collective-permute-start(bf16[1,64,1,128]{3,1,2,0:T(8,128)(2,1)S(1)} %copy-done.4), channel_id=1, source_target_pairs={{0,8},{8,16},{16,24},{24,32},{32,40},{40,48},{48,56},{56,64},{64,7... | collective-permute-start | bytes 49160 | tf_op jit(solution)/shard_map/ppermute | solution.py:16
  89.9 21.6 %collective-permute-start.21 = (bf16[1,64,1,128]{3,1,2,0:T(8,128)(2,1)S(1)}, bf16[1,64,1,128]{3,1,2,0:T(8,128)(2,1)S(1)}, u32[]{:S(2)}, u32[]{:S(2)}) collective-permute-start(bf16[1,64,1,128]{3,1,2,0:T(8,128)(2,1)S(1)} %copy-done.4), channel_id=1, source_target_pairs={{0,16},{8,24},{16,32},{24,40},{32,48},{40,56},{48,64},{56,72},{64,... | collective-permute-start | bytes 49160 | tf_op jit(solution)/shard_map/ppermute | solution.py:16
  96.6 34.5 %collective-permute-start.16 = (bf16[1,2048,1,128]{3,1,2,0:T(8,128)(2,1)S(1)}, bf16[1,2048,1,128]{3,1,2,0:T(8,128)(2,1)S(1)}, u32[]{:S(2)}, u32[]{:S(2)}) collective-permute-start(bf16[1,2048,1,128]{3,1,2,0:T(8,128)(2,1)S(1)} %copy-done.5), channel_id=1, source_target_pairs={{0,8},{8,16},{16,24},{24,32},{32,40},{40,48},{48,56},{56,64},{64,7... | collective-permute-start | bytes 1572872 | tf_op jit(solution)/shard_map/ppermute | solution.py:16
  100.5 16.8 %collective-permute-start.20 = (bf16[1,2048,1,128]{3,1,2,0:T(8,128)(2,1)S(1)}, bf16[1,2048,1,128]{3,1,2,0:T(8,128)(2,1)S(1)}, u32[]{:S(2)}, u32[]{:S(2)}) collective-permute-start(bf16[1,2048,1,128]{3,1,2,0:T(8,128)(2,1)S(1)} %copy-done.5), channel_id=1, source_target_pairs={{0,16},{8,24},{16,32},{24,40},{32,48},{40,56},{48,64},{56,72},{64,... | collective-permute-start | bytes 1572872 | tf_op jit(solution)/shard_map/ppermute | solution.py:16
  104.4 9.3 %collective-permute-start.23 = (bf16[1,64,1,128]{3,1,2,0:T(8,128)(2,1)S(1)}, bf16[1,64,1,128]{3,1,2,0:T(8,128)(2,1)S(1)}, u32[]{:S(2)}, u32[]{:S(2)}) collective-permute-start(bf16[1,64,1,128]{3,1,2,0:T(8,128)(2,1)S(1)} %copy-done.4), channel_id=1, source_target_pairs={{16,0},{24,8},{32,16},{40,24},{48,32},{56,40},{64,48},{72,56},{80,... | collective-permute-start | bytes 49160 | tf_op jit(solution)/shard_map/ppermute | solution.py:16
  111.5 17.7 %collective-permute-start.22 = (bf16[1,2048,1,128]{3,1,2,0:T(8,128)(2,1)S(1)}, bf16[1,2048,1,128]{3,1,2,0:T(8,128)(2,1)S(1)}, u32[]{:S(2)}, u32[]{:S(2)}) collective-permute-start(bf16[1,2048,1,128]{3,1,2,0:T(8,128)(2,1)S(1)} %copy-done.5), channel_id=1, source_target_pairs={{16,0},{24,8},{32,16},{40,24},{48,32},{56,40},{64,48},{72,56},{80,... | collective-permute-start | bytes 1572872 | tf_op jit(solution)/shard_map/ppermute | solution.py:16
  113.8 17.0 %collective-permute-start.19 = (bf16[1,64,1,128]{3,1,2,0:T(8,128)(2,1)S(1)}, bf16[1,64,1,128]{3,1,2,0:T(8,128)(2,1)S(1)}, u32[]{:S(2)}, u32[]{:S(2)}) collective-permute-start(bf16[1,64,1,128]{3,1,2,0:T(8,128)(2,1)S(1)} %copy-done.4), channel_id=1, source_target_pairs={{8,0},{16,8},{24,16},{32,24},{40,32},{48,40},{56,48},{64,56},{72,6... | collective-permute-start | bytes 49160 | tf_op jit(solution)/shard_map/ppermute | solution.py:16
  117.3 14.9 %collective-permute-start.18 = (bf16[1,2048,1,128]{3,1,2,0:T(8,128)(2,1)S(1)}, bf16[1,2048,1,128]{3,1,2,0:T(8,128)(2,1)S(1)}, u32[]{:S(2)}, u32[]{:S(2)}) collective-permute-start(bf16[1,2048,1,128]{3,1,2,0:T(8,128)(2,1)S(1)} %copy-done.5), channel_id=1, source_target_pairs={{8,0},{16,8},{24,16},{32,24},{40,32},{48,40},{56,48},{64,56},{72,6... | collective-permute-start | bytes 1572872 | tf_op jit(solution)/shard_map/ppermute | solution.py:16
  134.6 266.9 %reduce-scatter.4.cloned.1.call-start = ((), (), s32[]{:S(2)}) async-start(), calls=%async_computation.2 | async-start | bytes 1179648
  (8 other events, 463.2 us)
Sparse Core Ops, SparseCore 0:
  134.7 142.5 all-gather.1
  285.6 115.8 reduce-scatter.3
where the time goes:
time: 411 us; the launch traced here: 410 us
  waiting for transfers between devices  279 us (68%)
  starting transfers between devices  80.1 us (19%)
  matrix products  20.1 us (5%)
  between operations  17.7 us (4%)
  other arithmetic  8.27 us (2%)
  local copies, waits for them, and re-layouts  4.81 us (1%)
    all_gather x1, waiting for transfers between devices, body(): lax.all_gather(attended, 'thread', axis=0, tiled=True)  143 us
    unnamed x3, waiting for transfers between devices  116 us
    ppermute x24, starting transfers between devices, from_behind(): lax.ppermute(value, axis, [(source, source + steps) for source in range(f...  80.1 us
    ppermute x24, waiting for transfers between devices, from_behind(): lax.ppermute(value, axis, [(source, source + steps) for source in range(f...  20.3 us
  transfers between devices with their start and end apart: 26, of which 9 were waited for; matrix products, arithmetic and copies ran while one was open for 5% of the time, Pallas kernels for 0%

commit v1 on v0

v1 whole, which is shorter than its diff:
```python
import functools

import jax
import jax.numpy as jnp
from jax import lax
from jax.experimental import pallas as pl
from jax.experimental.pallas import tpu as pltpu
from jax.sharding import PartitionSpec as P

STEP_TOK = 16
NEGATIVE = -1e30
LOG2_E = 1.4426950408889634
VMEM_LIMIT = 40 * 1024 * 1024

FINE = (("zh", 4), ("zl", 2), ("x", 4), ("c", 2), ("w", 2), ("y", 4))
THREAD = ("zh", "zl", "x", "c")
HEAD = ("w", "y")

BLOCK = 256
PAD = 16
LANES = 128


def diagonal(size):
    rows = lax.broadcasted_iota(jnp.int32, (size, size), 0)
    return rows == lax.broadcasted_iota(jnp.int32, (size, size), 1)


def attend_block(queries, first_row, keys, values, fresh_keys, fresh_values, length, is_own):
    factor = queries.shape[1] ** (-0.5)
    contract = (((1,), (1,)), ((), ()))
    cached = lax.dot_general(queries, keys, contract, preferred_element_type=jnp.float32)
    fresh = lax.dot_general(queries, fresh_keys, contract, preferred_element_type=jnp.float32)
    position = lax.broadcasted_iota(jnp.int32, cached.shape, 1)
    cached = jnp.where(position < length, cached, NEGATIVE)
    new_count = fresh.shape[1]
    token = (first_row + lax.broadcasted_iota(jnp.int32, fresh.shape, 0)) % new_count
    key_token = lax.broadcasted_iota(jnp.int32, fresh.shape, 1)
    if is_own:
        allowed = key_token <= token
    else:
        allowed = key_token // STEP_TOK < token // STEP_TOK
    fresh = jnp.where(allowed, fresh, NEGATIVE)
    row_max = jnp.maximum(
        jnp.max(cached, axis=1, keepdims=True), jnp.max(fresh, axis=1, keepdims=True)
    )
    cached = jnp.exp2((cached - row_max) * (factor * LOG2_E))
    fresh = jnp.exp2((fresh - row_max) * (factor * LOG2_E))
    total = jnp.sum(cached, axis=1, keepdims=True) + jnp.sum(fresh, axis=1, keepdims=True)
    summed = jnp.dot(cached.astype(jnp.bfloat16), values, preferred_element_type=jnp.float32)
    summed += jnp.dot(fresh.astype(jnp.bfloat16), fresh_values, preferred_element_type=jnp.float32)
    return summed / total, row_max * factor + jnp.log(total)


def own_kernel(length_ref, query_ref, key_ref, value_ref, new_key_ref, new_value_ref, out_ref, log_ref):
    for start in range(0, out_ref.shape[0], BLOCK):
        block = pl.ds(start, BLOCK)
        result, log_total = attend_block(
            query_ref[block], start, key_ref[...], value_ref[...], new_key_ref[...],
            new_value_ref[...], length_ref[0], True,
        )
        out_ref[block] = result
        log_ref[block] = jnp.broadcast_to(log_total, result.shape)


def same_request(own_ref, other_ref):
    return jnp.max(jnp.abs(own_ref[...].astype(jnp.float32) - other_ref[...].astype(jnp.float32))) == 0.0


def near_kernel(
    length_ref, own_tag_ref, key_ref, value_ref, new_key_ref, new_value_ref, *refs
):
    count = len(refs) // 2
    rows = refs[0].shape[0] - PAD
    for query_ref, out_ref in zip(refs[:count], refs[count:]):
        sibling = same_request(own_tag_ref, query_ref.at[pl.ds(rows, PAD)])

        @pl.when(sibling)
        def _():
            lines = []
            for start in range(0, rows, BLOCK):
                result, log_total = attend_block(
                    query_ref[pl.ds(start, BLOCK)], start, key_ref[...], value_ref[...],
                    new_key_ref[...], new_value_ref[...], length_ref[0], False,
                )
                out_ref[pl.ds(start, BLOCK)] = result.astype(out_ref.dtype)
                for piece in range(0, BLOCK, LANES):
                    column = jnp.broadcast_to(log_total[piece : piece + LANES], (LANES, LANES))
                    lines.append(
                        jnp.sum(jnp.where(diagonal(LANES), column, 0.0), axis=0, keepdims=True)
                    )
            exact = jnp.concatenate(lines, axis=0)
            high = exact.astype(jnp.bfloat16).astype(jnp.float32)
            middle = (exact - high).astype(jnp.bfloat16).astype(jnp.float32)
            low = exact - high - middle
            parts = jnp.concatenate([high, middle, low, jnp.zeros_like(low)], axis=0)
            out_ref[pl.ds(rows, PAD)] = parts.astype(out_ref.dtype)

        @pl.when(jnp.logical_not(sibling))
        def _():
            out_ref[...] = jnp.zeros_like(out_ref)


def merge_kernel(own_tag_ref, own_ref, own_log_ref, *refs):
    count = (len(refs) - 1) // 2
    tag_refs, part_refs, out_ref = refs[:count], refs[count:-1], refs[-1]
    rows = own_ref.shape[0]
    tokens = out_ref.shape[0]
    lines = rows // LANES
    siblings, logs = [], []
    for tag_ref, part_ref in zip(tag_refs, part_refs):
        siblings.append(same_request(own_tag_ref, tag_ref))
        pieces = part_ref[pl.ds(rows, PAD)].astype(jnp.float32)
        exact = pieces[:lines] + pieces[lines : 2 * lines] + pieces[2 * lines : 3 * lines]
        logs.append(jnp.where(siblings[-1], exact, NEGATIVE))
    for line in range(lines):
        block = pl.ds(line * LANES, LANES)
        columns = [own_log_ref[block]]
        terms = [own_ref[block]]
        for sibling, log_total, part_ref in zip(siblings, logs, part_refs):
            spread = jnp.broadcast_to(log_total[line : line + 1], (LANES, LANES))
            column = jnp.sum(jnp.where(diagonal(LANES), spread, 0.0), axis=1, keepdims=True)
            columns.append(jnp.broadcast_to(column, (LANES, LANES)))
            terms.append(jnp.where(sibling, part_ref[block].astype(jnp.float32), 0.0))
        largest = functools.reduce(jnp.maximum, columns)
        shares = [jnp.exp(column - largest) for column in columns]
        total = functools.reduce(jnp.add, shares)
        summed = functools.reduce(jnp.add, [share * term for share, term in zip(shares, terms)])
        merged = (summed / total).astype(out_ref.dtype)
        for piece in range(0, LANES, tokens):
            group = (line * LANES + piece) // tokens
            out_ref[:, pl.ds(group * LANES, LANES)] = merged[piece : piece + tokens]


def project_kernel(core_ref, near_ref, far_ref, weight_ref, out_ref):
    threads, tokens, feats = near_ref.shape
    y_size, w_size, z_size = out_ref.shape[:3]
    piece = tokens // (y_size * w_size)
    span = threads * piece
    for features, core in ((near_ref, core_ref[0]), (far_ref, 1 - core_ref[0])):
        place = pl.ds(pl.multiple_of(core * span, span), span)
        lines = features[...].reshape(threads * tokens, feats)
        for pair in range(0, z_size, 2):
            weights = jnp.concatenate([weight_ref[pair], weight_ref[pair + 1]], axis=1)
            terms = jnp.dot(lines, weights, preferred_element_type=jnp.float32)
            terms = terms.reshape(threads, w_size, y_size, piece, 2 * LANES)
            for y in range(y_size):
                for w in range(w_size):
                    part = terms[:, w, y].reshape(span, 2 * LANES).astype(out_ref.dtype)
                    out_ref[y, w, pair, place] = part[:, :LANES]
                    out_ref[y, w, pair + 1, place] = part[:, LANES:]


def on_chip(count):
    return [pl.BlockSpec(memory_space=pltpu.VMEM)] * count


SCALAR = pl.BlockSpec(memory_space=pltpu.SMEM)
PARAMS = pltpu.CompilerParams(vmem_limit_bytes=VMEM_LIMIT)


def neighbours():
    count = 1
    for name in THREAD:
        count *= lax.axis_size(name)
    up = [(i, i + 2) for i in range(count - 2)]
    down = [(i + 2, i) for i in range(count - 2)]
    across = [pair for i in range(1, count - 1, 2) for pair in ((i, i + 1), (i + 1, i))]
    beside = [pair for i in range(0, count, 2) for pair in ((i, i + 1), (i + 1, i))]
    return (up, down, across, beside), (1, 0, 2, 3)


def project(attended, out_weight, weights):
    tokens, feats = attended.shape
    y_size, w_size, z_size = lax.axis_size("y"), lax.axis_size("w"), lax.axis_size("zh")
    threads, cores = lax.axis_size("zl") * lax.axis_size("x"), lax.axis_size("c")
    piece = tokens // (y_size * w_size)
    spread = jnp.broadcast_to(attended[None], (threads, tokens, feats))
    near = lax.all_to_all(spread, ("zl", "x"), 0, 0)
    far = lax.ppermute(near, "c", [(0, 1), (1, 0)])
    core = lax.axis_index("c").astype(jnp.int32).reshape(1)
    columns = out_weight.shape[1]
    terms = pl.pallas_call(
        project_kernel,
        out_shape=jax.ShapeDtypeStruct(
            (y_size, w_size, z_size, cores * threads * piece, columns), jnp.bfloat16
        ),
        in_specs=[SCALAR] + on_chip(3),
        out_specs=on_chip(1)[0],
        compiler_params=PARAMS,
        name="project",
    )(core, near, far, weights)
    terms = lax.all_to_all(terms, "y", 0, 0)
    terms = jnp.sum(terms.astype(jnp.float32), axis=0).astype(jnp.bfloat16)
    terms = lax.all_to_all(
        terms.reshape((w_size * z_size,) + terms.shape[2:]), ("w", "zh"), 0, 0
    ).reshape(terms.shape)
    result = jnp.sum(terms.astype(jnp.float32), axis=0).astype(jnp.bfloat16)
    result = result.reshape(z_size, cores, threads, piece, columns).transpose(0, 2, 1, 3, 4)
    return result.reshape(z_size * threads * cores, piece, columns)


def body(request_id, cache_len, query, new_key, new_value, key_cache, value_cache, out_weight):
    new_count, group_size, head_dim = query.shape[1:]
    rows = new_count * group_size
    weights = lax.all_gather(out_weight, "zh", axis=0)
    by_head = query[0].transpose(1, 0, 2).reshape(rows, head_dim)
    tag = jnp.broadcast_to((request_id[0] + 1).astype(jnp.bfloat16), (PAD, head_dim))
    packed = jnp.concatenate([by_head, tag], axis=0)
    ways, back = neighbours()
    arrived = [lax.ppermute(packed, THREAD, way) for way in ways]
    caches = (key_cache[0, :, 0], value_cache[0, :, 0], new_key[0, :, 0], new_value[0, :, 0])
    own, own_log = pl.pallas_call(
        own_kernel,
        out_shape=[jax.ShapeDtypeStruct((rows, head_dim), jnp.float32)] * 2,
        in_specs=[SCALAR] + on_chip(5),
        out_specs=on_chip(2),
        compiler_params=PARAMS,
        name="own",
    )(cache_len, by_head, *caches)
    parts = pl.pallas_call(
        near_kernel,
        out_shape=[jax.ShapeDtypeStruct(packed.shape, jnp.bfloat16)] * len(ways),
        in_specs=[SCALAR] + on_chip(5 + len(ways)),
        out_specs=on_chip(len(ways)),
        compiler_params=PARAMS,
        name="near",
    )(cache_len, tag, *caches, *arrived)
    returned = [lax.ppermute(parts[back[way]], THREAD, ways[way]) for way in range(len(ways))]
    tags = [one[rows:] for one in arrived]
    attended = pl.pallas_call(
        merge_kernel,
        out_shape=jax.ShapeDtypeStruct((new_count, group_size * head_dim), jnp.bfloat16),
        in_specs=on_chip(3 + 2 * len(ways)),
        out_specs=on_chip(1)[0],
        compiler_params=PARAMS,
        name="merge",
    )(tag, own, own_log, *tags, *returned)
    return project(attended, out_weight, weights)


def solution(mesh):
    fine = jax.sharding.Mesh(
        mesh.devices.reshape([size for _, size in FINE]), [name for name, _ in FINE]
    )
    placed = (
        P(THREAD),
        P(THREAD),
        P(THREAD, None, HEAD, None),
        P(THREAD, None, HEAD, None),
        P(THREAD, None, HEAD, None),
        P(THREAD, None, HEAD, None),
        P(THREAD, None, HEAD, None),
        P(HEAD, THREAD),
    )
    return jax.shard_map(
        body, mesh=fine, in_specs=placed, out_specs=P(None, HEAD, THREAD), check_vma=False
    )
```

time: 411 us -> 177 us (0.43)
  waiting for transfers between devices: 279 us -> 69 us
  starting transfers between devices: 80.1 us -> 35.6 us
  blocking collectives: 0 us -> 44.4 us
  matrix products: 20.1 us -> 0 us
  other arithmetic: 8.27 us -> 0.25 us
  Pallas kernels: 0 us -> 6.86 us
    unnamed x3 -> x1, waiting for transfers between devices: 116 us -> 0.71 us
    all_gather x1, waiting for transfers between devices: 143 us -> 51.1 us  [body(): weights = lax.all_gather(out_weight, 'zh', axis=0)]
    ppermute x24 -> x9, starting transfers between devices: 80.1 us -> 29.7 us  [the longest x4 15.1 us: body(): lax.ppermute(parts[back[way]], THREAD, ways[way])]
    all_to_all x0 -> x2, blocking collectives: none -> 44.4 us  [the longest x1 25.4 us: project(): lax.all_to_all(terms.reshape((w_size * z_size,) + terms.shape[2:]), ('w',...]
    dot_general x21 -> x0, matrix products: 20.1 us -> none  [the longest x10 7.28 us: partial_block(): jnp.einsum('hrd,khd->hrk', queries, key_rows, preferred_element_type=jnp....]
    ppermute x24 -> x9, waiting for transfers between devices: 20.3 us -> 4.63 us  [the longest x4 4.62 us: body(): arrived = [lax.ppermute(packed, THREAD, way) for way in ways]]
    all_to_all x0 -> x1, waiting for transfers between devices: none -> 12.5 us  [project(): near = lax.all_to_all(spread, ('zl', 'x'), 0, 0)]
    pallas_call x0 -> x4, Pallas kernels: none -> 6.86 us  [the longest x1 2.76 us: body(): pl.pallas_call(near_kernel, out_shape=[jax.ShapeDtypeStruct(packed.shape,...]
  transfers between devices with their start and end apart: 26 -> 11, of which waited for: 9 -> 4; matrix products, arithmetic and copies ran while one was open for 5% -> 0% of each run, Pallas kernels for 0% -> 1%
where the time goes in v1:
time: 177 us; the launch traced here: 176 us
  waiting for transfers between devices  69 us (39%)
  blocking collectives  44.4 us (25%)
  starting transfers between devices  35.6 us (20%)
  between operations  15 us (8%)
  Pallas kernels  6.86 us (4%)
  local copies, waits for them, and re-layouts  5.03 us (3%)
    all_gather x1, waiting for transfers between devices, body(): weights = lax.all_gather(out_weight, 'zh', axis=0)  51.1 us
    all_to_all x1, blocking collectives, project(): lax.all_to_all(terms.reshape((w_size * z_size,) + terms.shape[2:]), ('w',...  25.4 us
    all_to_all x1, blocking collectives, project(): terms = lax.all_to_all(terms, 'y', 0, 0)  19 us
    ppermute x4, starting transfers between devices, body(): lax.ppermute(parts[back[way]], THREAD, ways[way])  15.1 us
    ppermute x4, starting transfers between devices, body(): arrived = [lax.ppermute(packed, THREAD, way) for way in ways]  12.7 us
    all_to_all x1, waiting for transfers between devices, project(): near = lax.all_to_all(spread, ('zl', 'x'), 0, 0)  12.5 us
    all_to_all x1, starting transfers between devices, project(): near = lax.all_to_all(spread, ('zl', 'x'), 0, 0)  5.86 us
    ppermute x4, waiting for transfers between devices, body(): arrived = [lax.ppermute(packed, THREAD, way) for way in ways]  4.62 us
  transfers between devices with their start and end apart: 11, of which 4 were waited for; matrix products, arithmetic and copies ran while one was open for 0% of the time, Pallas kernels for 1%

profile of v1, /device:TPU:6, one launch (start us, length us, event | category | flops | bytes accessed | tf_op | source)
XLA Modules:
  0.0 176.1 jit_solution(8207577448560589884)
XLA Ops:
  7.3 0.9 copy.13
  8.2 1.9 %collective-permute-start.3 = (bf16[528,128]{1,0:T(8,128)(2,1)S(1)}, bf16[528,128]{1,0:T(8,128)(2,1)S(1)}, u32[]{:S(2)}, u32[]{:S(2)}) collective-permute-start(bf16[528,128]{1,0:T(8,128)(2,1)S(1)} %concatenate.3), channel_id=1, source_target_pairs={{0,8},{8,0},{16,24},{24,16},{32,40},{40,32},{48,56},{56,48},{64,72... | collective-permute-start | bytes 405512 | tf_op jit(solution)/shard_map/ppermute | solution.py:211
  10.2 2.8 %collective-permute-start.2 = (bf16[528,128]{1,0:T(8,128)(2,1)S(1)}, bf16[528,128]{1,0:T(8,128)(2,1)S(1)}, u32[]{:S(2)}, u32[]{:S(2)}) collective-permute-start(bf16[528,128]{1,0:T(8,128)(2,1)S(1)} %concatenate.3), channel_id=1, source_target_pairs={{8,16},{16,8},{24,32},{32,24},{40,48},{48,40},{56,64},{64,56},{72,... | collective-permute-start | bytes 405512 | tf_op jit(solution)/shard_map/ppermute | solution.py:211
  13.0 2.4 %collective-permute-start.1 = (bf16[528,128]{1,0:T(8,128)(2,1)S(1)}, bf16[528,128]{1,0:T(8,128)(2,1)S(1)}, u32[]{:S(2)}, u32[]{:S(2)}) collective-permute-start(bf16[528,128]{1,0:T(8,128)(2,1)S(1)} %concatenate.3), channel_id=1, source_target_pairs={{16,0},{24,8},{32,16},{40,24},{48,32},{56,40},{64,48},{72,56},{80,... | collective-permute-start | bytes 405512 | tf_op jit(solution)/shard_map/ppermute | solution.py:211
  15.5 5.5 %collective-permute-start = (bf16[528,128]{1,0:T(8,128)(2,1)S(1)}, bf16[528,128]{1,0:T(8,128)(2,1)S(1)}, u32[]{:S(2)}, u32[]{:S(2)}) collective-permute-start(bf16[528,128]{1,0:T(8,128)(2,1)S(1)} %concatenate.3), channel_id=1, source_target_pairs={{0,16},{8,24},{16,32},{24,40},{32,48},{40,56},{48,64},{56,72},{64,... | collective-permute-start | bytes 405512 | tf_op jit(solution)/shard_map/ppermute | solution.py:211
  21.6 1.8 %collective-permute-done.1.refs_1_ = bf16[528,128]{1,0:T(8,128)(2,1)S(1)} collective-permute-done((bf16[528,128]{1,0:T(8,128)(2,1)S(1)}, bf16[528,128]{1,0:T(8,128)(2,1)S(1)}, u32[]{:S(2)}, u32[]{:S(2)}) %collective-permute-start.1) | collective-permute-done | bytes 135200 | tf_op jit(solution)/shard_map/ppermute | solution.py:211
  23.4 2.8 %collective-permute-done.refs_0_ = bf16[528,128]{1,0:T(8,128)(2,1)S(1)} collective-permute-done((bf16[528,128]{1,0:T(8,128)(2,1)S(1)}, bf16[528,128]{1,0:T(8,128)(2,1)S(1)}, u32[]{:S(2)}, u32[]{:S(2)}) %collective-permute-start) | collective-permute-done | bytes 135200 | tf_op jit(solution)/shard_map/ppermute | solution.py:211
  26.3 1.0 copy-done.1
  27.3 2.8 %near.1 = (bf16[528,128]{1,0:T(8,128)(2,1)S(1)}, bf16[528,128]{1,0:T(8,128)(2,1)S(1)}, bf16[528,128]{1,0:T(8,128)(2,1)S(1)}, bf16[528,128]{1,0:T(8,128)(2,1)S(1)}) custom-call(s32[1]{0:T(128)S(6)} %copy.16.length_ref, bf16[16,128]{1,0:T(8,128)(2,1)S(1)} %broadcast_in_dim.4.own_tag_ref, bf16[2048,128]{1,0:T(8,128)(2,1)S(1)} %bitcast.17, ...), custom_call_target="tpu_custom_call" | custom-call | tf_op jit(solution)/shard_map/near/pallas_call | solution.py:221
  30.1 4.9 %collective-permute-start.4 = (bf16[528,128]{1,0:T(8,128)(2,1)S(1)}, bf16[528,128]{1,0:T(8,128)(2,1)S(1)}, u32[]{:S(2)}, u32[]{:S(2)}) collective-permute-start(bf16[528,128]{1,0:T(8,128)(2,1)S(1)} %get-tuple-element.13), channel_id=1, source_target_pairs={{0,16},{8,24},{16,32},{24,40},{32,48},{40,56},{48,64},{56,72},{64,... | collective-permute-start | bytes 405512 | tf_op jit(solution)/shard_map/ppermute | solution.py:229
  35.0 3.1 %collective-permute-start.5 = (bf16[528,128]{1,0:T(8,128)(2,1)S(1)}, bf16[528,128]{1,0:T(8,128)(2,1)S(1)}, u32[]{:S(2)}, u32[]{:S(2)}) collective-permute-start(bf16[528,128]{1,0:T(8,128)(2,1)S(1)} %get-tuple-element.14), channel_id=1, source_target_pairs={{16,0},{24,8},{32,16},{40,24},{48,32},{56,40},{64,48},{72,56},{80,... | collective-permute-start | bytes 405512 | tf_op jit(solution)/shard_map/ppermute | solution.py:229
  38.2 1.9 %collective-permute-start.6 = (bf16[528,128]{1,0:T(8,128)(2,1)S(1)}, bf16[528,128]{1,0:T(8,128)(2,1)S(1)}, u32[]{:S(2)}, u32[]{:S(2)}) collective-permute-start(bf16[528,128]{1,0:T(8,128)(2,1)S(1)} %get-tuple-element.15), channel_id=1, source_target_pairs={{8,16},{16,8},{24,32},{32,24},{40,48},{48,40},{56,64},{64,56},{72,... | collective-permute-start | bytes 405512 | tf_op jit(solution)/shard_map/ppermute | solution.py:229
  40.1 5.1 %collective-permute-start.7 = (bf16[528,128]{1,0:T(8,128)(2,1)S(1)}, bf16[528,128]{1,0:T(8,128)(2,1)S(1)}, u32[]{:S(2)}, u32[]{:S(2)}) collective-permute-start(bf16[528,128]{1,0:T(8,128)(2,1)S(1)} %get-tuple-element.16), channel_id=1, source_target_pairs={{0,8},{8,0},{16,24},{24,16},{32,40},{40,32},{48,56},{56,48},{64,72... | collective-permute-start | bytes 405512 | tf_op jit(solution)/shard_map/ppermute | solution.py:229
  45.2 2.2 %own.1 = (f32[512,128]{1,0:T(8,128)S(1)}, f32[512,128]{1,0:T(8,128)S(1)}) custom-call(s32[1]{0:T(128)S(6)} %copy.16.length_ref, bf16[512,128]{1,0:T(8,128)(2,1)S(1)} %bitcast.22, bf16[2048,128]{1,0:T(8,128)(2,1)S(1)} %bitcast.18, bf16[2048,128]{1,0:T(8,128)(2,1)S(1)} %bitcast.20, bf16[64,128]{1,0:T(8,128)(2,1)S(1)} %bitcast.25, bf16[64,128]{1,0:T(8,128)(2,1)S(1)} %bitcast.27), custom_call_target="tpu_custom_call" | custom-call | tf_op jit(solution)/shard_map/own/pallas_call | solution.py:213
  48.1 1.1 broadcast_in_dim.10
  49.2 5.9 %all-to-all-start = ((bf16[8,64,1024]{2,1,0:T(8,128)(2,1)}), bf16[8,64,1024]{2,1,0:T(8,128)(2,1)S(1)}, u32[]{:S(2)}, u32[]{:S(2)}) async-start(bf16[8,64,1024]{2,1,0:T(8,128)(2,1)} %broadcast_in_dim.10), calls=%async_computation | async-start | bytes 2097152 | tf_op jit(solution)/shard_map/all_to_all | solution.py:179
  55.1 0.7 all-gather.3.cloned.1.call-update
  55.8 12.5 %all-to-all-done.near_ref = bf16[8,64,1024]{2,1,0:T(8,128)(2,1)S(1)} async-done(((bf16[8,64,1024]{2,1,0:T(8,128)(2,1)}), bf16[8,64,1024]{2,1,0:T(8,128)(2,1)S(1)}, u32[]{:S(2)}, u32[]{:S(2)}) %all-to-all-start) | async-done | bytes 1048608 | tf_op jit(solution)/shard_map/all_to_all | solution.py:179
  68.4 1.9 %collective-permute-start.8 = (bf16[8,64,1024]{2,1,0:T(8,128)(2,1)S(1)}, bf16[8,64,1024]{2,1,0:T(8,128)(2,1)S(1)}, u32[]{:S(2)}, u32[]{:S(2)}) collective-permute-start(bf16[8,64,1024]{2,1,0:T(8,128)(2,1)S(1)} %all-to-all-done.near_ref), channel_id=1, source_target_pairs={{0,8},{8,0},{1,9},{9,1},{2,10},{10,2},{3,11},{11,3},{4,12},{12,4},... | collective-permute-start | bytes 3145736 | tf_op jit(solution)/shard_map/ppermute | solution.py:180
  70.3 51.1 %all-gather.3.cloned.1.call-done = bf16[4096,128]{1,0:T(8,128)(2,1)} async-done(((bf16[1024,128]{1,0:T(8,128)(2,1)}), bf16[4096,128]{1,0:T(8,128)(2,1)}) %all-gather.3.cloned.1.call-update) | async-done | bytes 1048592 | tf_op jit(solution)/shard_map/all_gather | solution.py:206
  121.4 1.2 copy-done.3
  122.6 1.3 project.1
  123.9 19.0 %all_to_all.15 = bf16[4,2,4,128,128]{4,3,2,1,0:T(8,128)(2,1)S(1)} all-to-all(bf16[4,2,4,128,128]{4,3,2,1,0:T(8,128)(2,1)S(1)} %project.1), channel_id=1, replica_groups=mesh['zh'=4,'zl'=2,'x'=4,'c'=2,'w'=2,'y'=4] {'y'}, dimensions={0} | all-to-all | bytes 2097152 | tf_op jit(solution)/shard_map/all_to_all | solution.py:193
  143.0 25.4 %all_to_all.16 = bf16[8,128,128]{2,1,0:T(8,128)(2,1)S(1)} all-to-all(bf16[8,128,128]{2,1,0:T(8,128)(2,1)S(1)} %bitcast.28), channel_id=1, replica_groups=mesh['zh'=4,'zl'=2,'x'=4,'c'=2,'w'=2,'y'=4] {'w','zh'}, dimensions={0} | all-to-all | bytes 524288 | tf_op jit(solution)/shard_map/all_to_all | solution.py:195
  (28 shorter events, 1.6 us)
Async XLA Ops:
  6.5 19.7 %copy-start = (bf16[1,2048,1,128]{3,1,2,0:T(8,128)(2,1)S(1)}, bf16[1,2048,1,128]{3,1,2,0:T(8,128)(2,1)}, u32[]{:S(2)}) copy-start(bf16[1,2048,1,128]{3,1,2,0:T(8,128)(2,1)} %param.13) | copy-start | bytes 1572868
  8.2 18.1 %copy-start.4 = (bf16[1,64,1,128]{3,1,2,0:T(8,128)(2,1)S(1)}, bf16[1,64,1,128]{3,1,2,0:T(8,128)(2,1)}, u32[]{:S(2)}) copy-start(bf16[1,64,1,128]{3,1,2,0:T(8,128)(2,1)} %param.11) | copy-start | bytes 49156
  8.2 18.1 %copy-start.5 = (bf16[1,64,1,128]{3,1,2,0:T(8,128)(2,1)S(1)}, bf16[1,64,1,128]{3,1,2,0:T(8,128)(2,1)}, u32[]{:S(2)}) copy-start(bf16[1,64,1,128]{3,1,2,0:T(8,128)(2,1)} %param.12) | copy-start | bytes 49156
  8.2 13.4 %collective-permute-start.3 = (bf16[528,128]{1,0:T(8,128)(2,1)S(1)}, bf16[528,128]{1,0:T(8,128)(2,1)S(1)}, u32[]{:S(2)}, u32[]{:S(2)}) collective-permute-start(bf16[528,128]{1,0:T(8,128)(2,1)S(1)} %concatenate.3), channel_id=1, source_target_pairs={{0,8},{8,0},{16,24},{24,16},{32,40},{40,32},{48,56},{56,48},{64,72... | collective-permute-start | bytes 405512 | tf_op jit(solution)/shard_map/ppermute | solution.py:211
  10.2 11.5 %collective-permute-start.2 = (bf16[528,128]{1,0:T(8,128)(2,1)S(1)}, bf16[528,128]{1,0:T(8,128)(2,1)S(1)}, u32[]{:S(2)}, u32[]{:S(2)}) collective-permute-start(bf16[528,128]{1,0:T(8,128)(2,1)S(1)} %concatenate.3), channel_id=1, source_target_pairs={{8,16},{16,8},{24,32},{32,24},{40,48},{48,40},{56,64},{64,56},{72,... | collective-permute-start | bytes 405512 | tf_op jit(solution)/shard_map/ppermute | solution.py:211
  13.0 10.4 %collective-permute-start.1 = (bf16[528,128]{1,0:T(8,128)(2,1)S(1)}, bf16[528,128]{1,0:T(8,128)(2,1)S(1)}, u32[]{:S(2)}, u32[]{:S(2)}) collective-permute-start(bf16[528,128]{1,0:T(8,128)(2,1)S(1)} %concatenate.3), channel_id=1, source_target_pairs={{16,0},{24,8},{32,16},{40,24},{48,32},{56,40},{64,48},{72,56},{80,... | collective-permute-start | bytes 405512 | tf_op jit(solution)/shard_map/ppermute | solution.py:211
  15.5 10.8 %collective-permute-start = (bf16[528,128]{1,0:T(8,128)(2,1)S(1)}, bf16[528,128]{1,0:T(8,128)(2,1)S(1)}, u32[]{:S(2)}, u32[]{:S(2)}) collective-permute-start(bf16[528,128]{1,0:T(8,128)(2,1)S(1)} %concatenate.3), channel_id=1, source_target_pairs={{0,16},{8,24},{16,32},{24,40},{32,48},{40,56},{48,64},{56,72},{64,... | collective-permute-start | bytes 405512 | tf_op jit(solution)/shard_map/ppermute | solution.py:211
  26.3 1.0 copy-start.1
  27.3 17.9 %copy-start.2 = (bf16[1,2048,1,128]{3,1,2,0:T(8,128)(2,1)S(1)}, bf16[1,2048,1,128]{3,1,2,0:T(8,128)(2,1)}, u32[]{:S(2)}) copy-start(bf16[1,2048,1,128]{3,1,2,0:T(8,128)(2,1)} %param.14) | copy-start | bytes 1572868
  30.1 17.4 %collective-permute-start.4 = (bf16[528,128]{1,0:T(8,128)(2,1)S(1)}, bf16[528,128]{1,0:T(8,128)(2,1)S(1)}, u32[]{:S(2)}, u32[]{:S(2)}) collective-permute-start(bf16[528,128]{1,0:T(8,128)(2,1)S(1)} %get-tuple-element.13), channel_id=1, source_target_pairs={{0,16},{8,24},{16,32},{24,40},{32,48},{40,56},{48,64},{56,72},{64,... | collective-permute-start | bytes 405512 | tf_op jit(solution)/shard_map/ppermute | solution.py:229
  35.0 12.5 %collective-permute-start.5 = (bf16[528,128]{1,0:T(8,128)(2,1)S(1)}, bf16[528,128]{1,0:T(8,128)(2,1)S(1)}, u32[]{:S(2)}, u32[]{:S(2)}) collective-permute-start(bf16[528,128]{1,0:T(8,128)(2,1)S(1)} %get-tuple-element.14), channel_id=1, source_target_pairs={{16,0},{24,8},{32,16},{40,24},{48,32},{56,40},{64,48},{72,56},{80,... | collective-permute-start | bytes 405512 | tf_op jit(solution)/shard_map/ppermute | solution.py:229
  38.2 9.4 %collective-permute-start.6 = (bf16[528,128]{1,0:T(8,128)(2,1)S(1)}, bf16[528,128]{1,0:T(8,128)(2,1)S(1)}, u32[]{:S(2)}, u32[]{:S(2)}) collective-permute-start(bf16[528,128]{1,0:T(8,128)(2,1)S(1)} %get-tuple-element.15), channel_id=1, source_target_pairs={{8,16},{16,8},{24,32},{32,24},{40,48},{48,40},{56,64},{64,56},{72,... | collective-permute-start | bytes 405512 | tf_op jit(solution)/shard_map/ppermute | solution.py:229
  40.1 7.4 %collective-permute-start.7 = (bf16[528,128]{1,0:T(8,128)(2,1)S(1)}, bf16[528,128]{1,0:T(8,128)(2,1)S(1)}, u32[]{:S(2)}, u32[]{:S(2)}) collective-permute-start(bf16[528,128]{1,0:T(8,128)(2,1)S(1)} %get-tuple-element.16), channel_id=1, source_target_pairs={{0,8},{8,0},{16,24},{24,16},{32,40},{40,32},{48,56},{56,48},{64,72... | collective-permute-start | bytes 405512 | tf_op jit(solution)/shard_map/ppermute | solution.py:229
  49.2 19.1 %all-to-all-start = ((bf16[8,64,1024]{2,1,0:T(8,128)(2,1)}), bf16[8,64,1024]{2,1,0:T(8,128)(2,1)S(1)}, u32[]{:S(2)}, u32[]{:S(2)}) async-start(bf16[8,64,1024]{2,1,0:T(8,128)(2,1)} %broadcast_in_dim.10), calls=%async_computation | async-start | bytes 2097152 | tf_op jit(solution)/shard_map/all_to_all | solution.py:179
  55.1 66.3 %all-gather.3.cloned.1.call-start = ((), (), s32[]{:S(2)}) async-start(), calls=%async_computation.3 | async-start | bytes 1310720 | tf_op jit(solution)/shard_map/all_gather | solution.py:206
  68.4 53.0 %collective-permute-start.8 = (bf16[8,64,1024]{2,1,0:T(8,128)(2,1)S(1)}, bf16[8,64,1024]{2,1,0:T(8,128)(2,1)S(1)}, u32[]{:S(2)}, u32[]{:S(2)}) collective-permute-start(bf16[8,64,1024]{2,1,0:T(8,128)(2,1)S(1)} %all-to-all-done.near_ref), channel_id=1, source_target_pairs={{0,8},{8,0},{1,9},{9,1},{2,10},{10,2},{3,11},{11,3},{4,12},{12,4},... | collective-permute-start | bytes 3145736 | tf_op jit(solution)/shard_map/ppermute | solution.py:180
  121.4 1.2 copy-start.3
Sparse Core Ops, SparseCore 0:
  58.0 63.2 all-gather.2

commit v2 on v1

--- a/solution.py
+++ b/solution.py
@@ -12,8 +12,8 @@
 LOG2_E = 1.4426950408889634
 VMEM_LIMIT = 40 * 1024 * 1024
 
-FINE = (("zh", 4), ("zl", 2), ("x", 4), ("c", 2), ("w", 2), ("y", 4))
-THREAD = ("zh", "zl", "x", "c")
+FINE = (("zt", 2), ("zm", 2), ("zl", 2), ("x", 4), ("c", 2), ("w", 2), ("y", 4))
+THREAD = ("zt", "zm", "zl", "x", "c")
 HEAD = ("w", "y")
 
 BLOCK = 256
@@ -52,7 +52,21 @@
     return summed / total, row_max * factor + jnp.log(total)
 
 
-def own_kernel(length_ref, query_ref, key_ref, value_ref, new_key_ref, new_value_ref, out_ref, log_ref):
+def load(pairs, sems):
+    copies = [pltpu.make_async_copy(src, dst, sems.at[i]) for i, (src, dst) in enumerate(pairs)]
+    for copy in copies:
+        copy.start()
+    return copies
+
+
+def own_kernel(
+    length_ref, query_ref, key_hbm, value_hbm, new_key_hbm, new_value_hbm, out_ref, log_ref,
+    key_ref, value_ref, new_key_ref, new_value_ref, sems,
+):
+    for copy in load(
+        ((key_hbm, key_ref), (value_hbm, value_ref), (new_key_hbm, new_key_ref), (new_value_hbm, new_value_ref)), sems
+    ):
+        copy.wait()
     for start in range(0, out_ref.shape[0], BLOCK):
         block = pl.ds(start, BLOCK)
         result, log_total = attend_block(
@@ -67,9 +81,12 @@
     return jnp.max(jnp.abs(own_ref[...].astype(jnp.float32) - other_ref[...].astype(jnp.float32))) == 0.0
 
 
-def near_kernel(
-    length_ref, own_tag_ref, key_ref, value_ref, new_key_ref, new_value_ref, *refs
-):
+def near_kernel(length_ref, own_tag_ref, key_hbm, value_hbm, new_key_hbm, new_value_hbm, *refs):
+    *refs, key_ref, value_ref, new_key_ref, new_value_ref, sems = refs
+    for copy in load(
+        ((key_hbm, key_ref), (value_hbm, value_ref), (new_key_hbm, new_key_ref), (new_value_hbm, new_value_ref)), sems
+    ):
+        copy.wait()
     count = len(refs) // 2
     rows = refs[0].shape[0] - PAD
     for query_ref, out_ref in zip(refs[:count], refs[count:]):
@@ -101,9 +118,13 @@
             out_ref[...] = jnp.zeros_like(out_ref)
 
 
-def merge_kernel(own_tag_ref, own_ref, own_log_ref, *refs):
-    count = (len(refs) - 1) // 2
-    tag_refs, part_refs, out_ref = refs[:count], refs[count:-1], refs[-1]
+def merge_kernel(ways, own_tag_ref, own_ref, own_log_ref, *refs):
+    tag_refs, part_refs, weight_refs = refs[:ways], refs[ways : 2 * ways], refs[2 * ways : -3]
+    out_ref, stack_ref, sems = refs[-3:]
+    copies = load(
+        [(ref, stack_ref.at[copy, i]) for copy in range(stack_ref.shape[0]) for i, ref in enumerate(weight_refs)],
+        sems,
+    )
     rows = own_ref.shape[0]
     tokens = out_ref.shape[0]
     lines = rows // LANES
@@ -130,31 +151,36 @@
         for piece in range(0, LANES, tokens):
             group = (line * LANES + piece) // tokens
             out_ref[:, pl.ds(group * LANES, LANES)] = merged[piece : piece + tokens]
-
-
-def project_kernel(core_ref, near_ref, far_ref, weight_ref, out_ref):
-    threads, tokens, feats = near_ref.shape
-    y_size, w_size, z_size = out_ref.shape[:3]
+    for copy in copies:
+        copy.wait()
+
+
+def project_kernel(place_ref, weight_ref, *refs):
+    piece_refs, (out_ref, lines_ref) = refs[:-2], refs[-2:]
+    pieces, (tokens, feats) = len(piece_refs), piece_refs[0].shape
+    y_size, w_size = out_ref.shape[2:4]
     piece = tokens // (y_size * w_size)
-    span = threads * piece
-    for features, core in ((near_ref, core_ref[0]), (far_ref, 1 - core_ref[0])):
-        place = pl.ds(pl.multiple_of(core * span, span), span)
-        lines = features[...].reshape(threads * tokens, feats)
-        for pair in range(0, z_size, 2):
-            weights = jnp.concatenate([weight_ref[pair], weight_ref[pair + 1]], axis=1)
-            terms = jnp.dot(lines, weights, preferred_element_type=jnp.float32)
-            terms = terms.reshape(threads, w_size, y_size, piece, 2 * LANES)
-            for y in range(y_size):
-                for w in range(w_size):
-                    part = terms[:, w, y].reshape(span, 2 * LANES).astype(out_ref.dtype)
-                    out_ref[y, w, pair, place] = part[:, :LANES]
-                    out_ref[y, w, pair + 1, place] = part[:, LANES:]
+    span = pieces * piece
+    for index, piece_ref in enumerate(piece_refs):
+        first = pl.multiple_of((place_ref[0] ^ index) * tokens, tokens)
+        lines_ref[pl.ds(first, tokens)] = piece_ref[...]
+    for x in range(weight_ref.shape[0]):
+        weights = jnp.concatenate([weight_ref[x, 0], weight_ref[x, 1]], axis=1)
+        terms = jnp.dot(lines_ref[...], weights, preferred_element_type=jnp.float32)
+        terms = terms.reshape(pieces, w_size, y_size, piece, 2 * LANES)
+        for y in range(y_size):
+            for w in range(w_size):
+                far = place_ref[2] ^ w
+                part = terms[:, w, y].reshape(span, 2 * LANES).astype(out_ref.dtype)
+                for side in range(2):
+                    out_ref[place_ref[1] ^ side ^ far, x, y, far] = part[:, side * LANES : (side + 1) * LANES]
 
 
 def on_chip(count):
     return [pl.BlockSpec(memory_space=pltpu.VMEM)] * count
 
 
+IN_HBM = pl.BlockSpec(memory_space=pltpu.HBM)
 SCALAR = pl.BlockSpec(memory_space=pltpu.SMEM)
 PARAMS = pltpu.CompilerParams(vmem_limit_bytes=VMEM_LIMIT)
 
@@ -170,73 +196,91 @@
     return (up, down, across, beside), (1, 0, 2, 3)
 
 
-def project(attended, out_weight, weights):
-    tokens, feats = attended.shape
-    y_size, w_size, z_size = lax.axis_size("y"), lax.axis_size("w"), lax.axis_size("zh")
-    threads, cores = lax.axis_size("zl") * lax.axis_size("x"), lax.axis_size("c")
-    piece = tokens // (y_size * w_size)
-    spread = jnp.broadcast_to(attended[None], (threads, tokens, feats))
-    near = lax.all_to_all(spread, ("zl", "x"), 0, 0)
-    far = lax.ppermute(near, "c", [(0, 1), (1, 0)])
-    core = lax.axis_index("c").astype(jnp.int32).reshape(1)
-    columns = out_weight.shape[1]
+def swap(value, axis, bit):
+    names = (axis,) if isinstance(axis, str) else axis
+    count = 1
+    for name in names:
+        count *= lax.axis_size(name)
+    return lax.ppermute(value, axis, [(i, i ^ bit) for i in range(count)])
+
+
+def project(attended, stack):
+    tokens = attended.shape[0]
+    size = {name: count for name, count in FINE}
+    at = {name: lax.axis_index(name) for name in size}
+    weights = lax.all_to_all(stack, "x", 0, 0)
+    over_t, over_m = swap(attended, "zt", 1), swap(attended, "zm", 1)
+    near = (attended, over_m, over_t, swap(over_t, "zm", 1))
+    pieces = [piece for one in near for piece in (one, swap(one, "c", 1))]
+    place = jnp.stack([at["zt"] * 4 + at["zm"] * 2 + at["c"], at["zl"], at["w"]]).astype(jnp.int32)
+    piece, columns = tokens // (size["y"] * size["w"]), weights.shape[-1]
+    block = (size["zl"], size["x"], size["y"], size["w"], len(pieces) * piece, columns)
     terms = pl.pallas_call(
         project_kernel,
-        out_shape=jax.ShapeDtypeStruct(
-            (y_size, w_size, z_size, cores * threads * piece, columns), jnp.bfloat16
-        ),
-        in_specs=[SCALAR] + on_chip(3),
+        out_shape=jax.ShapeDtypeStruct(block, jnp.bfloat16),
+        in_specs=[SCALAR] + on_chip(1 + len(pieces)),
         out_specs=on_chip(1)[0],
+        scratch_shapes=[pltpu.VMEM((len(pieces) * tokens, attended.shape[1]), jnp.bfloat16)],
         compiler_params=PARAMS,
         name="project",
-    )(core, near, far, weights)
-    terms = lax.all_to_all(terms, "y", 0, 0)
-    terms = jnp.sum(terms.astype(jnp.float32), axis=0).astype(jnp.bfloat16)
-    terms = lax.all_to_all(
-        terms.reshape((w_size * z_size,) + terms.shape[2:]), ("w", "zh"), 0, 0
-    ).reshape(terms.shape)
-    result = jnp.sum(terms.astype(jnp.float32), axis=0).astype(jnp.bfloat16)
-    result = result.reshape(z_size, cores, threads, piece, columns).transpose(0, 2, 1, 3, 4)
-    return result.reshape(z_size * threads * cores, piece, columns)
+    )(place, weights, *pieces)
+    terms = lax.all_to_all(terms.reshape((-1,) + block[3:]), ("zl", "x", "y"), 0, 0).reshape(block)
+    terms = jnp.sum(terms.astype(jnp.float32), axis=2)
+    arrived = swap(terms[:, :, 1].astype(jnp.bfloat16), ("zl", "w"), 3)
+    result = (terms[:, :, 0] + arrived.astype(jnp.float32)).astype(jnp.bfloat16)
+    result = result.reshape(
+        size["zl"], size["x"], size["zt"], size["zm"], size["c"], piece, columns
+    )
+    return result.transpose(2, 3, 0, 1, 4, 5, 6).reshape(-1, piece, columns)
 
 
 def body(request_id, cache_len, query, new_key, new_value, key_cache, value_cache, out_weight):
     new_count, group_size, head_dim = query.shape[1:]
     rows = new_count * group_size
-    weights = lax.all_gather(out_weight, "zh", axis=0)
     by_head = query[0].transpose(1, 0, 2).reshape(rows, head_dim)
     tag = jnp.broadcast_to((request_id[0] + 1).astype(jnp.bfloat16), (PAD, head_dim))
     packed = jnp.concatenate([by_head, tag], axis=0)
     ways, back = neighbours()
     arrived = [lax.ppermute(packed, THREAD, way) for way in ways]
     caches = (key_cache[0, :, 0], value_cache[0, :, 0], new_key[0, :, 0], new_value[0, :, 0])
+    cache_space = [pltpu.VMEM(one.shape, one.dtype) for one in caches]
+    cache_space.append(pltpu.SemaphoreType.DMA((len(caches),)))
     own, own_log = pl.pallas_call(
         own_kernel,
         out_shape=[jax.ShapeDtypeStruct((rows, head_dim), jnp.float32)] * 2,
-        in_specs=[SCALAR] + on_chip(5),
+        in_specs=[SCALAR] + on_chip(1) + [IN_HBM] * 4,
         out_specs=on_chip(2),
+        scratch_shapes=cache_space,
         compiler_params=PARAMS,
         name="own",
     )(cache_len, by_head, *caches)
+    weights = (out_weight, swap(out_weight, "zl", 1))
     parts = pl.pallas_call(
         near_kernel,
         out_shape=[jax.ShapeDtypeStruct(packed.shape, jnp.bfloat16)] * len(ways),
-        in_specs=[SCALAR] + on_chip(5 + len(ways)),
+        in_specs=[SCALAR] + on_chip(1) + [IN_HBM] * 4 + on_chip(len(ways)),
         out_specs=on_chip(len(ways)),
+        scratch_shapes=cache_space,
         compiler_params=PARAMS,
         name="near",
     )(cache_len, tag, *caches, *arrived)
     returned = [lax.ppermute(parts[back[way]], THREAD, ways[way]) for way in range(len(ways))]
     tags = [one[rows:] for one in arrived]
-    attended = pl.pallas_call(
-        merge_kernel,
-        out_shape=jax.ShapeDtypeStruct((new_count, group_size * head_dim), jnp.bfloat16),
-        in_specs=on_chip(3 + 2 * len(ways)),
-        out_specs=on_chip(1)[0],
+    attended, stack = pl.pallas_call(
+        functools.partial(merge_kernel, len(ways)),
+        out_shape=[
+            jax.ShapeDtypeStruct((new_count, group_size * head_dim), jnp.bfloat16),
+            jax.ShapeDtypeStruct(
+                (lax.axis_size("x"), len(weights)) + out_weight.shape, out_weight.dtype
+            ),
+        ],
+        in_specs=on_chip(3 + 2 * len(ways) + len(weights)),
+        out_specs=on_chip(1) + [IN_HBM],
+        scratch_shapes=[pltpu.SemaphoreType.DMA((lax.axis_size("x") * len(weights),))],
         compiler_params=PARAMS,
         name="merge",
-    )(tag, own, own_log, *tags, *returned)
-    return project(attended, out_weight, weights)
+    )(tag, own, own_log, *tags, *returned, *weights)
+    return project(attended, stack)
 
 
 def solution(mesh):

time: 177 us -> 136 us (0.77)
  the two profiles are of different devices: /device:TPU:6 before, /device:TPU:163 now
where the time goes in v2:
time: 136 us
  starting transfers between devices  66.8 us (49%)
  waiting for transfers between devices  26.1 us (19%)
  blocking collectives  24 us (18%)
  Pallas kernels  10.2 us (7%)
  local copies, waits for them, and re-layouts  6.48 us (5%)
  between operations  1.7 us (1%)
    ppermute x9, starting transfers between devices, swap(): return lax.ppermute(value, axis, [(i, i ^ bit) for i in range(count)])  33.7 us
    ppermute x9, waiting for transfers between devices, swap(): return lax.ppermute(value, axis, [(i, i ^ bit) for i in range(count)])  24.5 us
    all_to_all x1, blocking collectives, project(): lax.all_to_all(terms.reshape((-1,) + block[3:]), ('zl', 'x', 'y'), 0, 0)  24 us
    ppermute x4, starting transfers between devices, body(): lax.ppermute(parts[back[way]], THREAD, ways[way])  16.3 us
    ppermute x4, starting transfers between devices, body(): arrived = [lax.ppermute(packed, THREAD, way) for way in ways]  10.9 us
    all_to_all x1, starting transfers between devices, project(): weights = lax.all_to_all(stack, 'x', 0, 0)  5.98 us
    pallas_call x1, Pallas kernels, body(): pl.pallas_call(near_kernel, out_shape=[jax.ShapeDtypeStruct(packed.shape,...  5.1 us
    unnamed x12, local copies, waits for them, and re-layouts  4.85 us
  transfers between devices with their start and end apart: 18, of which 4 were waited for; matrix products, arithmetic and copies ran while one was open for 0% of the time, Pallas kernels for 5%

profile of v2, /device:TPU:163, one launch (start us, length us, event | category | flops | bytes accessed | tf_op | source)
XLA Modules:
  0.0 135.6 jit_solution(3129605723799487066)
XLA Ops:
  1.7 2.6 %collective-permute-start.3 = (bf16[528,128]{1,0:T(8,128)(2,1)S(1)}, bf16[528,128]{1,0:T(8,128)(2,1)S(1)}, u32[]{:S(2)}, u32[]{:S(2)}) collective-permute-start(bf16[528,128]{1,0:T(8,128)(2,1)S(1)} %concatenate.3), channel_id=1, source_target_pairs={{0,8},{8,0},{16,24},{24,16},{32,40},{40,32},{48,56},{56,48},{64,72... | collective-permute-start | bytes 405512 | tf_op jit(solution)/shard_map/ppermute | solution.py:244
  4.2 3.0 %collective-permute-start.2 = (bf16[528,128]{1,0:T(8,128)(2,1)S(1)}, bf16[528,128]{1,0:T(8,128)(2,1)S(1)}, u32[]{:S(2)}, u32[]{:S(2)}) collective-permute-start(bf16[528,128]{1,0:T(8,128)(2,1)S(1)} %concatenate.3), channel_id=1, source_target_pairs={{8,16},{16,8},{24,32},{32,24},{40,48},{48,40},{56,64},{64,56},{72,... | collective-permute-start | bytes 405512 | tf_op jit(solution)/shard_map/ppermute | solution.py:244
  7.3 2.2 %collective-permute-start.1 = (bf16[528,128]{1,0:T(8,128)(2,1)S(1)}, bf16[528,128]{1,0:T(8,128)(2,1)S(1)}, u32[]{:S(2)}, u32[]{:S(2)}) collective-permute-start(bf16[528,128]{1,0:T(8,128)(2,1)S(1)} %concatenate.3), channel_id=1, source_target_pairs={{16,0},{24,8},{32,16},{40,24},{48,32},{56,40},{64,48},{72,56},{80,... | collective-permute-start | bytes 405512 | tf_op jit(solution)/shard_map/ppermute | solution.py:244
  9.4 3.1 %collective-permute-start = (bf16[528,128]{1,0:T(8,128)(2,1)S(1)}, bf16[528,128]{1,0:T(8,128)(2,1)S(1)}, u32[]{:S(2)}, u32[]{:S(2)}) collective-permute-start(bf16[528,128]{1,0:T(8,128)(2,1)S(1)} %concatenate.3), channel_id=1, source_target_pairs={{0,16},{8,24},{16,32},{24,40},{32,48},{40,56},{48,64},{56,72},{64,... | collective-permute-start | bytes 405512 | tf_op jit(solution)/shard_map/ppermute | solution.py:244
  12.6 1.9 %collective-permute-start.8 = (bf16[1024,128]{1,0:T(8,128)(2,1)}, bf16[1024,128]{1,0:T(8,128)(2,1)S(1)}, u32[]{:S(2)}, u32[]{:S(2)}) collective-permute-start(bf16[1024,128]{1,0:T(8,128)(2,1)} %refs_8_.1), channel_id=1, source_target_pairs={{0,64},{64,0},{1,65},{65,1},{2,66},{66,2},{3,67},{67,3},{4,68},{68... | collective-permute-start | bytes 786440 | tf_op jit(solution)/shard_map/ppermute | solution.py:204
  20.2 5.1 %near.1 = (bf16[528,128]{1,0:T(8,128)(2,1)S(1)}, bf16[528,128]{1,0:T(8,128)(2,1)S(1)}, bf16[528,128]{1,0:T(8,128)(2,1)S(1)}, bf16[528,128]{1,0:T(8,128)(2,1)S(1)}) custom-call(s32[1]{0:T(128)S(6)} %copy.19.length_ref, bf16[16,128]{1,0:T(8,128)(2,1)S(1)} %broadcast_in_dim.3.own_tag_ref, bf16[2048,128]{1,0:T(8,128)(2,1)S(1)} %bitcast.31, ...), custom_call_target="tpu_custom_call" | custom-call | tf_op jit(solution)/shard_map/near/pallas_call | solution.py:258
  25.3 2.9 %collective-permute-start.4 = (bf16[528,128]{1,0:T(8,128)(2,1)S(1)}, bf16[528,128]{1,0:T(8,128)(2,1)S(1)}, u32[]{:S(2)}, u32[]{:S(2)}) collective-permute-start(bf16[528,128]{1,0:T(8,128)(2,1)S(1)} %get-tuple-element.15), channel_id=1, source_target_pairs={{0,16},{8,24},{16,32},{24,40},{32,48},{40,56},{48,64},{56,72},{64,... | collective-permute-start | bytes 405512 | tf_op jit(solution)/shard_map/ppermute | solution.py:267
  28.2 5.5 %collective-permute-start.5 = (bf16[528,128]{1,0:T(8,128)(2,1)S(1)}, bf16[528,128]{1,0:T(8,128)(2,1)S(1)}, u32[]{:S(2)}, u32[]{:S(2)}) collective-permute-start(bf16[528,128]{1,0:T(8,128)(2,1)S(1)} %get-tuple-element.16), channel_id=1, source_target_pairs={{16,0},{24,8},{32,16},{40,24},{48,32},{56,40},{64,48},{72,56},{80,... | collective-permute-start | bytes 405512 | tf_op jit(solution)/shard_map/ppermute | solution.py:267
  33.7 1.9 %collective-permute-start.6 = (bf16[528,128]{1,0:T(8,128)(2,1)S(1)}, bf16[528,128]{1,0:T(8,128)(2,1)S(1)}, u32[]{:S(2)}, u32[]{:S(2)}) collective-permute-start(bf16[528,128]{1,0:T(8,128)(2,1)S(1)} %get-tuple-element.17), channel_id=1, source_target_pairs={{8,16},{16,8},{24,32},{32,24},{40,48},{48,40},{56,64},{64,56},{72,... | collective-permute-start | bytes 405512 | tf_op jit(solution)/shard_map/ppermute | solution.py:267
  35.6 6.0 %collective-permute-start.7 = (bf16[528,128]{1,0:T(8,128)(2,1)S(1)}, bf16[528,128]{1,0:T(8,128)(2,1)S(1)}, u32[]{:S(2)}, u32[]{:S(2)}) collective-permute-start(bf16[528,128]{1,0:T(8,128)(2,1)S(1)} %get-tuple-element.18), channel_id=1, source_target_pairs={{0,8},{8,0},{16,24},{24,16},{32,40},{40,32},{48,56},{56,48},{64,72... | collective-permute-start | bytes 405512 | tf_op jit(solution)/shard_map/ppermute | solution.py:267
  41.6 2.4 %own.1 = (f32[512,128]{1,0:T(8,128)S(1)}, f32[512,128]{1,0:T(8,128)S(1)}) custom-call(s32[1]{0:T(128)S(6)} %copy.19.length_ref, bf16[512,128]{1,0:T(8,128)(2,1)S(1)} %bitcast.36, bf16[2048,128]{1,0:T(8,128)(2,1)S(1)} %bitcast.32, bf16[2048,128]{1,0:T(8,128)(2,1)S(1)} %bitcast.34, bf16[64,128]{1,0:T(8,128)(2,1)S(1)} %bitcast.38, bf16[64,128]{1,0:T(8,128)(2,1)S(1)} %bitcast.40), custom_call_target="tpu_custom_call" | custom-call | tf_op jit(solution)/shard_map/own/pallas_call | solution.py:248
  46.3 6.0 %all-to-all-start = ((bf16[4,2,1024,128]{3,2,1,0:T(8,128)(2,1)}), bf16[4,2,1024,128]{3,2,1,0:T(8,128)(2,1)S(1)}, u32[]{:S(2)}, u32[]{:S(2)}) async-start(bf16[4,2,1024,128]{3,2,1,0:T(8,128)(2,1)} %copy-done), calls=%async_computation | async-start | bytes 4194304 | tf_op jit(solution)/shard_map/all_to_all | solution.py:211
  52.3 1.9 %collective-permute-start.12 = (bf16[64,1024]{1,0:T(8,128)(2,1)S(1)}, bf16[64,1024]{1,0:T(8,128)(2,1)S(1)}, u32[]{:S(2)}, u32[]{:S(2)}) collective-permute-start(bf16[64,1024]{1,0:T(8,128)(2,1)S(1)} %get-tuple-element.20.refs_0_), channel_id=1, source_target_pairs={{0,256},{256,0},{1,257},{257,1},{2,258},{258,2},{3,259},{259,3},{4... | collective-permute-start | bytes 393224 | tf_op jit(solution)/shard_map/ppermute | solution.py:204
  54.2 6.2 %collective-permute-start.10 = (bf16[64,1024]{1,0:T(8,128)(2,1)S(1)}, bf16[64,1024]{1,0:T(8,128)(2,1)S(1)}, u32[]{:S(2)}, u32[]{:S(2)}) collective-permute-start(bf16[64,1024]{1,0:T(8,128)(2,1)S(1)} %get-tuple-element.20.refs_0_), channel_id=1, source_target_pairs={{0,128},{128,0},{1,129},{129,1},{2,130},{130,2},{3,131},{131,3},{4... | collective-permute-start | bytes 393224 | tf_op jit(solution)/shard_map/ppermute | solution.py:204
  60.4 6.8 %collective-permute-done.12.refs_4_ = bf16[64,1024]{1,0:T(8,128)(2,1)S(1)} collective-permute-done((bf16[64,1024]{1,0:T(8,128)(2,1)S(1)}, bf16[64,1024]{1,0:T(8,128)(2,1)S(1)}, u32[]{:S(2)}, u32[]{:S(2)}) %collective-permute-start.12) | collective-permute-done | bytes 131104 | tf_op jit(solution)/shard_map/ppermute | solution.py:204
  67.2 7.9 %collective-permute-start.14 = (bf16[64,1024]{1,0:T(8,128)(2,1)S(1)}, bf16[64,1024]{1,0:T(8,128)(2,1)S(1)}, u32[]{:S(2)}, u32[]{:S(2)}) collective-permute-start(bf16[64,1024]{1,0:T(8,128)(2,1)S(1)} %collective-permute-done.12.refs_4_), channel_id=1, source_target_pairs={{0,128},{128,0},{1,129},{129,1},{2,130},{130,2},{3,131},{131,3},{4... | collective-permute-start | bytes 393224 | tf_op jit(solution)/shard_map/ppermute | solution.py:204
  75.2 2.9 %collective-permute-start.9 = (bf16[64,1024]{1,0:T(8,128)(2,1)S(1)}, bf16[64,1024]{1,0:T(8,128)(2,1)S(1)}, u32[]{:S(2)}, u32[]{:S(2)}) collective-permute-start(bf16[64,1024]{1,0:T(8,128)(2,1)S(1)} %get-tuple-element.20.refs_0_), channel_id=1, source_target_pairs={{0,8},{8,0},{1,9},{9,1},{2,10},{10,2},{3,11},{11,3},{4,12},{12,4},... | collective-permute-start | bytes 393224 | tf_op jit(solution)/shard_map/ppermute | solution.py:204
  78.1 1.9 %collective-permute-start.13 = (bf16[64,1024]{1,0:T(8,128)(2,1)S(1)}, bf16[64,1024]{1,0:T(8,128)(2,1)S(1)}, u32[]{:S(2)}, u32[]{:S(2)}) collective-permute-start(bf16[64,1024]{1,0:T(8,128)(2,1)S(1)} %collective-permute-done.12.refs_4_), channel_id=1, source_target_pairs={{0,8},{8,0},{1,9},{9,1},{2,10},{10,2},{3,11},{11,3},{4,12},{12,4},... | collective-permute-start | bytes 393224 | tf_op jit(solution)/shard_map/ppermute | solution.py:204
  80.1 2.4 %collective-permute-start.11 = (bf16[64,1024]{1,0:T(8,128)(2,1)S(1)}, bf16[64,1024]{1,0:T(8,128)(2,1)S(1)}, u32[]{:S(2)}, u32[]{:S(2)}) collective-permute-start(bf16[64,1024]{1,0:T(8,128)(2,1)S(1)} %collective-permute-done.10.refs_2_), channel_id=1, source_target_pairs={{0,8},{8,0},{1,9},{9,1},{2,10},{10,2},{3,11},{11,3},{4,12},{12,4},... | collective-permute-start | bytes 393224 | tf_op jit(solution)/shard_map/ppermute | solution.py:204
  82.5 1.9 %collective-permute-start.15 = (bf16[64,1024]{1,0:T(8,128)(2,1)S(1)}, bf16[64,1024]{1,0:T(8,128)(2,1)S(1)}, u32[]{:S(2)}, u32[]{:S(2)}) collective-permute-start(bf16[64,1024]{1,0:T(8,128)(2,1)S(1)} %collective-permute-done.14.refs_6_), channel_id=1, source_target_pairs={{0,8},{8,0},{1,9},{9,1},{2,10},{10,2},{3,11},{11,3},{4,12},{12,4},... | collective-permute-start | bytes 393224 | tf_op jit(solution)/shard_map/ppermute | solution.py:204
  85.7 1.9 %project.1 = bf16[2,4,4,2,64,128]{5,4,3,2,1,0:T(8,128)(2,1)S(1)} custom-call(s32[3]{0:T(128)S(1)} %pad_add_fusion.place_ref, bf16[4,2,1024,128]{3,2,1,0:T(8,128)(2,1)S(1)} %all-to-all-done.weight_ref, bf16[64,1024]{1,0:T(8,128)(2,1)S(1)} %get-tuple-element.20.refs_0_, bf16[64,1024]{1,0:T(8,128)(2,1)S(1)} %collective-permute-done.9.refs_1_, ...), custom_call_target="tpu_custom_call" | custom-call | tf_op jit(solution)/shard_map/project/pallas_call | solution.py:218
  87.6 24.0 %all_to_all.10 = bf16[32,2,64,128]{3,2,1,0:T(8,128)(2,1)S(1)} all-to-all(bf16[32,2,64,128]{3,2,1,0:T(8,128)(2,1)S(1)} %bitcast.30), channel_id=1, replica_groups=mesh['zt'=2,'zm'=2,'zl'=2,'x'=4,'c'=2,'w'=2,'y'=4] {'zl','x','y'}, dimensions={0} | all-to-all | bytes 2097152 | tf_op jit(solution)/shard_map/all_to_all | solution.py:227
  111.9 6.5 %collective-permute-start.16 = (bf16[2,4,64,128]{3,2,1,0:T(8,128)(2,1)S(1)}, bf16[2,4,64,128]{3,2,1,0:T(8,128)(2,1)S(1)}, u32[]{:S(2)}, u32[]{:S(2)}) collective-permute-start(bf16[2,4,64,128]{3,2,1,0:T(8,128)(2,1)S(1)} %fusion.2), channel_id=1, source_target_pairs={{0,68},{4,64},{64,4},{68,0},{1,69},{5,65},{65,5},{69,1},{2,70},{6,... | collective-permute-start | bytes 393224 | tf_op jit(solution)/shard_map/ppermute | solution.py:204
  118.3 16.5 %collective-permute-done.16 = bf16[2,4,64,128]{3,2,1,0:T(8,128)(2,1)S(1)} collective-permute-done((bf16[2,4,64,128]{3,2,1,0:T(8,128)(2,1)S(1)}, bf16[2,4,64,128]{3,2,1,0:T(8,128)(2,1)S(1)}, u32[]{:S(2)}, u32[]{:S(2)}) %collective-permute-start.16) | collective-permute-done | bytes 131104 | tf_op jit(solution)/shard_map/ppermute | solution.py:204
  (41 shorter events, 10.4 us)
Async XLA Ops:
  0.0 44.1 %copy-start.3 = (bf16[1024,128]{1,0:T(8,128)(2,1)S(1)}, bf16[1024,128]{1,0:T(8,128)(2,1)}, u32[]{:S(2)}) copy-start(bf16[1024,128]{1,0:T(8,128)(2,1)} %refs_8_.1) | copy-start | bytes 786436
  1.7 13.5 %collective-permute-start.3 = (bf16[528,128]{1,0:T(8,128)(2,1)S(1)}, bf16[528,128]{1,0:T(8,128)(2,1)S(1)}, u32[]{:S(2)}, u32[]{:S(2)}) collective-permute-start(bf16[528,128]{1,0:T(8,128)(2,1)S(1)} %concatenate.3), channel_id=1, source_target_pairs={{0,8},{8,0},{16,24},{24,16},{32,40},{40,32},{48,56},{56,48},{64,72... | collective-permute-start | bytes 405512 | tf_op jit(solution)/shard_map/ppermute | solution.py:244
  4.2 10.9 %collective-permute-start.2 = (bf16[528,128]{1,0:T(8,128)(2,1)S(1)}, bf16[528,128]{1,0:T(8,128)(2,1)S(1)}, u32[]{:S(2)}, u32[]{:S(2)}) collective-permute-start(bf16[528,128]{1,0:T(8,128)(2,1)S(1)} %concatenate.3), channel_id=1, source_target_pairs={{8,16},{16,8},{24,32},{32,24},{40,48},{48,40},{56,64},{64,56},{72,... | collective-permute-start | bytes 405512 | tf_op jit(solution)/shard_map/ppermute | solution.py:244
  7.3 7.9 %collective-permute-start.1 = (bf16[528,128]{1,0:T(8,128)(2,1)S(1)}, bf16[528,128]{1,0:T(8,128)(2,1)S(1)}, u32[]{:S(2)}, u32[]{:S(2)}) collective-permute-start(bf16[528,128]{1,0:T(8,128)(2,1)S(1)} %concatenate.3), channel_id=1, source_target_pairs={{16,0},{24,8},{32,16},{40,24},{48,32},{56,40},{64,48},{72,56},{80,... | collective-permute-start | bytes 405512 | tf_op jit(solution)/shard_map/ppermute | solution.py:244
  9.4 7.3 %collective-permute-start = (bf16[528,128]{1,0:T(8,128)(2,1)S(1)}, bf16[528,128]{1,0:T(8,128)(2,1)S(1)}, u32[]{:S(2)}, u32[]{:S(2)}) collective-permute-start(bf16[528,128]{1,0:T(8,128)(2,1)S(1)} %concatenate.3), channel_id=1, source_target_pairs={{0,16},{8,24},{16,32},{24,40},{32,48},{40,56},{48,64},{56,72},{64,... | collective-permute-start | bytes 405512 | tf_op jit(solution)/shard_map/ppermute | solution.py:244
  12.6 31.5 %collective-permute-start.8 = (bf16[1024,128]{1,0:T(8,128)(2,1)}, bf16[1024,128]{1,0:T(8,128)(2,1)S(1)}, u32[]{:S(2)}, u32[]{:S(2)}) collective-permute-start(bf16[1024,128]{1,0:T(8,128)(2,1)} %refs_8_.1), channel_id=1, source_target_pairs={{0,64},{64,0},{1,65},{65,1},{2,66},{66,2},{3,67},{67,3},{4,68},{68... | collective-permute-start | bytes 786440 | tf_op jit(solution)/shard_map/ppermute | solution.py:204
  16.7 1.0 copy-start.1
  17.7 1.0 copy-start.2
  18.8 0.7 copy-start.4
  19.5 0.7 copy-start.5
  25.3 18.7 %collective-permute-start.4 = (bf16[528,128]{1,0:T(8,128)(2,1)S(1)}, bf16[528,128]{1,0:T(8,128)(2,1)S(1)}, u32[]{:S(2)}, u32[]{:S(2)}) collective-permute-start(bf16[528,128]{1,0:T(8,128)(2,1)S(1)} %get-tuple-element.15), channel_id=1, source_target_pairs={{0,16},{8,24},{16,32},{24,40},{32,48},{40,56},{48,64},{56,72},{64,... | collective-permute-start | bytes 405512 | tf_op jit(solution)/shard_map/ppermute | solution.py:267
  28.2 15.9 %collective-permute-start.5 = (bf16[528,128]{1,0:T(8,128)(2,1)S(1)}, bf16[528,128]{1,0:T(8,128)(2,1)S(1)}, u32[]{:S(2)}, u32[]{:S(2)}) collective-permute-start(bf16[528,128]{1,0:T(8,128)(2,1)S(1)} %get-tuple-element.16), channel_id=1, source_target_pairs={{16,0},{24,8},{32,16},{40,24},{48,32},{56,40},{64,48},{72,56},{80,... | collective-permute-start | bytes 405512 | tf_op jit(solution)/shard_map/ppermute | solution.py:267
  33.7 10.4 %collective-permute-start.6 = (bf16[528,128]{1,0:T(8,128)(2,1)S(1)}, bf16[528,128]{1,0:T(8,128)(2,1)S(1)}, u32[]{:S(2)}, u32[]{:S(2)}) collective-permute-start(bf16[528,128]{1,0:T(8,128)(2,1)S(1)} %get-tuple-element.17), channel_id=1, source_target_pairs={{8,16},{16,8},{24,32},{32,24},{40,48},{48,40},{56,64},{64,56},{72,... | collective-permute-start | bytes 405512 | tf_op jit(solution)/shard_map/ppermute | solution.py:267
  35.6 8.5 %collective-permute-start.7 = (bf16[528,128]{1,0:T(8,128)(2,1)S(1)}, bf16[528,128]{1,0:T(8,128)(2,1)S(1)}, u32[]{:S(2)}, u32[]{:S(2)}) collective-permute-start(bf16[528,128]{1,0:T(8,128)(2,1)S(1)} %get-tuple-element.18), channel_id=1, source_target_pairs={{0,8},{8,0},{16,24},{24,16},{32,40},{40,32},{48,56},{56,48},{64,72... | collective-permute-start | bytes 405512 | tf_op jit(solution)/shard_map/ppermute | solution.py:267
  45.0 1.3 copy-start
  46.3 39.4 %all-to-all-start = ((bf16[4,2,1024,128]{3,2,1,0:T(8,128)(2,1)}), bf16[4,2,1024,128]{3,2,1,0:T(8,128)(2,1)S(1)}, u32[]{:S(2)}, u32[]{:S(2)}) async-start(bf16[4,2,1024,128]{3,2,1,0:T(8,128)(2,1)} %copy-done), calls=%async_computation | async-start | bytes 4194304 | tf_op jit(solution)/shard_map/all_to_all | solution.py:211
  52.3 15.0 %collective-permute-start.12 = (bf16[64,1024]{1,0:T(8,128)(2,1)S(1)}, bf16[64,1024]{1,0:T(8,128)(2,1)S(1)}, u32[]{:S(2)}, u32[]{:S(2)}) collective-permute-start(bf16[64,1024]{1,0:T(8,128)(2,1)S(1)} %get-tuple-element.20.refs_0_), channel_id=1, source_target_pairs={{0,256},{256,0},{1,257},{257,1},{2,258},{258,2},{3,259},{259,3},{4... | collective-permute-start | bytes 393224 | tf_op jit(solution)/shard_map/ppermute | solution.py:204
  54.2 25.9 %collective-permute-start.10 = (bf16[64,1024]{1,0:T(8,128)(2,1)S(1)}, bf16[64,1024]{1,0:T(8,128)(2,1)S(1)}, u32[]{:S(2)}, u32[]{:S(2)}) collective-permute-start(bf16[64,1024]{1,0:T(8,128)(2,1)S(1)} %get-tuple-element.20.refs_0_), channel_id=1, source_target_pairs={{0,128},{128,0},{1,129},{129,1},{2,130},{130,2},{3,131},{131,3},{4... | collective-permute-start | bytes 393224 | tf_op jit(solution)/shard_map/ppermute | solution.py:204
  67.2 15.2 %collective-permute-start.14 = (bf16[64,1024]{1,0:T(8,128)(2,1)S(1)}, bf16[64,1024]{1,0:T(8,128)(2,1)S(1)}, u32[]{:S(2)}, u32[]{:S(2)}) collective-permute-start(bf16[64,1024]{1,0:T(8,128)(2,1)S(1)} %collective-permute-done.12.refs_4_), channel_id=1, source_target_pairs={{0,128},{128,0},{1,129},{129,1},{2,130},{130,2},{3,131},{131,3},{4... | collective-permute-start | bytes 393224 | tf_op jit(solution)/shard_map/ppermute | solution.py:204
  75.2 9.3 %collective-permute-start.9 = (bf16[64,1024]{1,0:T(8,128)(2,1)S(1)}, bf16[64,1024]{1,0:T(8,128)(2,1)S(1)}, u32[]{:S(2)}, u32[]{:S(2)}) collective-permute-start(bf16[64,1024]{1,0:T(8,128)(2,1)S(1)} %get-tuple-element.20.refs_0_), channel_id=1, source_target_pairs={{0,8},{8,0},{1,9},{9,1},{2,10},{10,2},{3,11},{11,3},{4,12},{12,4},... | collective-permute-start | bytes 393224 | tf_op jit(solution)/shard_map/ppermute | solution.py:204
  78.1 6.4 %collective-permute-start.13 = (bf16[64,1024]{1,0:T(8,128)(2,1)S(1)}, bf16[64,1024]{1,0:T(8,128)(2,1)S(1)}, u32[]{:S(2)}, u32[]{:S(2)}) collective-permute-start(bf16[64,1024]{1,0:T(8,128)(2,1)S(1)} %collective-permute-done.12.refs_4_), channel_id=1, source_target_pairs={{0,8},{8,0},{1,9},{9,1},{2,10},{10,2},{3,11},{11,3},{4,12},{12,4},... | collective-permute-start | bytes 393224 | tf_op jit(solution)/shard_map/ppermute | solution.py:204
  80.1 4.4 %collective-permute-start.11 = (bf16[64,1024]{1,0:T(8,128)(2,1)S(1)}, bf16[64,1024]{1,0:T(8,128)(2,1)S(1)}, u32[]{:S(2)}, u32[]{:S(2)}) collective-permute-start(bf16[64,1024]{1,0:T(8,128)(2,1)S(1)} %collective-permute-done.10.refs_2_), channel_id=1, source_target_pairs={{0,8},{8,0},{1,9},{9,1},{2,10},{10,2},{3,11},{11,3},{4,12},{12,4},... | collective-permute-start | bytes 393224 | tf_op jit(solution)/shard_map/ppermute | solution.py:204
  82.5 3.2 %collective-permute-start.15 = (bf16[64,1024]{1,0:T(8,128)(2,1)S(1)}, bf16[64,1024]{1,0:T(8,128)(2,1)S(1)}, u32[]{:S(2)}, u32[]{:S(2)}) collective-permute-start(bf16[64,1024]{1,0:T(8,128)(2,1)S(1)} %collective-permute-done.14.refs_6_), channel_id=1, source_target_pairs={{0,8},{8,0},{1,9},{9,1},{2,10},{10,2},{3,11},{11,3},{4,12},{12,4},... | collective-permute-start | bytes 393224 | tf_op jit(solution)/shard_map/ppermute | solution.py:204
  111.9 23.0 %collective-permute-start.16 = (bf16[2,4,64,128]{3,2,1,0:T(8,128)(2,1)S(1)}, bf16[2,4,64,128]{3,2,1,0:T(8,128)(2,1)S(1)}, u32[]{:S(2)}, u32[]{:S(2)}) collective-permute-start(bf16[2,4,64,128]{3,2,1,0:T(8,128)(2,1)S(1)} %fusion.2), channel_id=1, source_target_pairs={{0,68},{4,64},{64,4},{68,0},{1,69},{5,65},{65,5},{69,1},{2,70},{6,... | collective-permute-start | bytes 393224 | tf_op jit(solution)/shard_map/ppermute | solution.py:204

commit v3 on v2

--- a/solution.py
+++ b/solution.py
@@ -31,8 +31,8 @@
     contract = (((1,), (1,)), ((), ()))
     cached = lax.dot_general(queries, keys, contract, preferred_element_type=jnp.float32)
     fresh = lax.dot_general(queries, fresh_keys, contract, preferred_element_type=jnp.float32)
-    position = lax.broadcasted_iota(jnp.int32, cached.shape, 1)
-    cached = jnp.where(position < length, cached, NEGATIVE)
+    position = lax.broadcasted_iota(jnp.int32, (1, cached.shape[1]), 1)
+    cached = cached + jnp.where(position < length, 0.0, NEGATIVE)
     new_count = fresh.shape[1]
     token = (first_row + lax.broadcasted_iota(jnp.int32, fresh.shape, 0)) % new_count
     key_token = lax.broadcasted_iota(jnp.int32, fresh.shape, 1)
@@ -46,10 +46,12 @@
     )
     cached = jnp.exp2((cached - row_max) * (factor * LOG2_E))
     fresh = jnp.exp2((fresh - row_max) * (factor * LOG2_E))
-    total = jnp.sum(cached, axis=1, keepdims=True) + jnp.sum(fresh, axis=1, keepdims=True)
-    summed = jnp.dot(cached.astype(jnp.bfloat16), values, preferred_element_type=jnp.float32)
-    summed += jnp.dot(fresh.astype(jnp.bfloat16), fresh_values, preferred_element_type=jnp.float32)
-    return summed / total, row_max * factor + jnp.log(total)
+    wide = jnp.concatenate([values, jnp.ones_like(values)], axis=1)
+    summed = jnp.dot(cached.astype(jnp.bfloat16), wide, preferred_element_type=jnp.float32)
+    wide = jnp.concatenate([fresh_values, jnp.ones_like(fresh_values)], axis=1)
+    summed += jnp.dot(fresh.astype(jnp.bfloat16), wide, preferred_element_type=jnp.float32)
+    total = summed[:, LANES:]
+    return summed[:, :LANES] / total, row_max * factor + jnp.log(total)
 
 
 def load(pairs, sems):
@@ -74,7 +76,7 @@
             new_value_ref[...], length_ref[0], True,
         )
         out_ref[block] = result
-        log_ref[block] = jnp.broadcast_to(log_total, result.shape)
+        log_ref[block] = log_total
 
 
 def same_request(own_ref, other_ref):
@@ -102,7 +104,7 @@
                 )
                 out_ref[pl.ds(start, BLOCK)] = result.astype(out_ref.dtype)
                 for piece in range(0, BLOCK, LANES):
-                    column = jnp.broadcast_to(log_total[piece : piece + LANES], (LANES, LANES))
+                    column = log_total[piece : piece + LANES]
                     lines.append(
                         jnp.sum(jnp.where(diagonal(LANES), column, 0.0), axis=0, keepdims=True)
                     )
@@ -118,13 +120,9 @@
             out_ref[...] = jnp.zeros_like(out_ref)
 
 
-def merge_kernel(ways, own_tag_ref, own_ref, own_log_ref, *refs):
-    tag_refs, part_refs, weight_refs = refs[:ways], refs[ways : 2 * ways], refs[2 * ways : -3]
-    out_ref, stack_ref, sems = refs[-3:]
-    copies = load(
-        [(ref, stack_ref.at[copy, i]) for copy in range(stack_ref.shape[0]) for i, ref in enumerate(weight_refs)],
-        sems,
-    )
+def merge_kernel(own_tag_ref, own_ref, own_log_ref, *refs):
+    count = (len(refs) - 1) // 2
+    tag_refs, part_refs, out_ref = refs[:count], refs[count:-1], refs[-1]
     rows = own_ref.shape[0]
     tokens = out_ref.shape[0]
     lines = rows // LANES
@@ -151,8 +149,28 @@
         for piece in range(0, LANES, tokens):
             group = (line * LANES + piece) // tokens
             out_ref[:, pl.ds(group * LANES, LANES)] = merged[piece : piece + tokens]
-    for copy in copies:
+
+
+def copies_kernel(first_hbm, second_hbm, out_hbm, first_ref, second_ref, sems):
+    pair = (first_ref, second_ref)
+    for copy in load(((first_hbm, first_ref), (second_hbm, second_ref)), sems):
         copy.wait()
+    sent = load([(pair[i], out_hbm.at[copy, i]) for copy in range(out_hbm.shape[0]) for i in range(2)], sems)
+    for copy in sent:
+        copy.wait()
+
+
+def pack_kernel(request_ref, query_ref, packed_ref, tag_ref):
+    tokens, heads, _ = query_ref.shape
+    for head in range(heads):
+        packed_ref[pl.ds(head * tokens, tokens)] = query_ref[:, head]
+    tag = jnp.full(tag_ref.shape, request_ref[0] + 1, jnp.int32).astype(jnp.float32).astype(tag_ref.dtype)
+    packed_ref[pl.ds(heads * tokens, PAD)] = tag
+    tag_ref[...] = tag
+
+
+def relay_kernel(in_ref, out_ref):
+    out_ref[...] = in_ref[...]
 
 
 def project_kernel(place_ref, weight_ref, *refs):
@@ -182,6 +200,7 @@
 
 IN_HBM = pl.BlockSpec(memory_space=pltpu.HBM)
 SCALAR = pl.BlockSpec(memory_space=pltpu.SMEM)
+DEAR = pl.CostEstimate(flops=40_000_000_000, bytes_accessed=0, transcendentals=0)
 PARAMS = pltpu.CompilerParams(vmem_limit_bytes=VMEM_LIMIT)
 
 
@@ -189,11 +208,13 @@
     count = 1
     for name in THREAD:
         count *= lax.axis_size(name)
-    up = [(i, i + 2) for i in range(count - 2)]
-    down = [(i + 2, i) for i in range(count - 2)]
-    across = [pair for i in range(1, count - 1, 2) for pair in ((i, i + 1), (i + 1, i))]
-    beside = [pair for i in range(0, count, 2) for pair in ((i, i + 1), (i + 1, i))]
-    return (up, down, across, beside), (1, 0, 2, 3)
+    both = lambda pairs: [pair for i, j in pairs for pair in ((i, j), (j, i))]
+    return (
+        both((i, i + 2) for i in range(count) if i % 4 < 2),
+        both((i, i + 2) for i in range(count - 2) if i % 4 >= 2),
+        both((i, i + 1) for i in range(1, count - 1, 2)),
+        both((i, i + 1) for i in range(0, count, 2)),
+    )
 
 
 def swap(value, axis, bit):
@@ -210,6 +231,15 @@
     at = {name: lax.axis_index(name) for name in size}
     weights = lax.all_to_all(stack, "x", 0, 0)
     over_t, over_m = swap(attended, "zt", 1), swap(attended, "zm", 1)
+    over_t = pl.pallas_call(
+        relay_kernel,
+        out_shape=jax.ShapeDtypeStruct(over_t.shape, over_t.dtype),
+        in_specs=on_chip(1),
+        out_specs=on_chip(1)[0],
+        compiler_params=PARAMS,
+        cost_estimate=DEAR,
+        name="relay",
+    )(over_t)
     near = (attended, over_m, over_t, swap(over_t, "zm", 1))
     pieces = [piece for one in near for piece in (one, swap(one, "c", 1))]
     place = jnp.stack([at["zt"] * 4 + at["zm"] * 2 + at["c"], at["zl"], at["w"]]).astype(jnp.int32)
@@ -237,10 +267,19 @@
 def body(request_id, cache_len, query, new_key, new_value, key_cache, value_cache, out_weight):
     new_count, group_size, head_dim = query.shape[1:]
     rows = new_count * group_size
-    by_head = query[0].transpose(1, 0, 2).reshape(rows, head_dim)
-    tag = jnp.broadcast_to((request_id[0] + 1).astype(jnp.bfloat16), (PAD, head_dim))
-    packed = jnp.concatenate([by_head, tag], axis=0)
-    ways, back = neighbours()
+    packed, tag = pl.pallas_call(
+        pack_kernel,
+        out_shape=[
+            jax.ShapeDtypeStruct((rows + PAD, head_dim), jnp.bfloat16),
+            jax.ShapeDtypeStruct((PAD, head_dim), jnp.bfloat16),
+        ],
+        in_specs=[SCALAR] + on_chip(1),
+        out_specs=on_chip(2),
+        compiler_params=PARAMS,
+        cost_estimate=DEAR,
+        name="pack",
+    )(request_id, query[0])
+    ways = neighbours()
     arrived = [lax.ppermute(packed, THREAD, way) for way in ways]
     caches = (key_cache[0, :, 0], value_cache[0, :, 0], new_key[0, :, 0], new_value[0, :, 0])
     cache_space = [pltpu.VMEM(one.shape, one.dtype) for one in caches]
@@ -253,7 +292,7 @@
         scratch_shapes=cache_space,
         compiler_params=PARAMS,
         name="own",
-    )(cache_len, by_head, *caches)
+    )(cache_len, packed, *caches)
     weights = (out_weight, swap(out_weight, "zl", 1))
     parts = pl.pallas_call(
         near_kernel,
@@ -264,22 +303,26 @@
         compiler_params=PARAMS,
         name="near",
     )(cache_len, tag, *caches, *arrived)
-    returned = [lax.ppermute(parts[back[way]], THREAD, ways[way]) for way in range(len(ways))]
+    returned = [lax.ppermute(part, THREAD, way) for part, way in zip(parts, ways)]
     tags = [one[rows:] for one in arrived]
-    attended, stack = pl.pallas_call(
-        functools.partial(merge_kernel, len(ways)),
-        out_shape=[
-            jax.ShapeDtypeStruct((new_count, group_size * head_dim), jnp.bfloat16),
-            jax.ShapeDtypeStruct(
-                (lax.axis_size("x"), len(weights)) + out_weight.shape, out_weight.dtype
-            ),
-        ],
-        in_specs=on_chip(3 + 2 * len(ways) + len(weights)),
-        out_specs=on_chip(1) + [IN_HBM],
-        scratch_shapes=[pltpu.SemaphoreType.DMA((lax.axis_size("x") * len(weights),))],
+    attended = pl.pallas_call(
+        merge_kernel,
+        out_shape=jax.ShapeDtypeStruct((new_count, group_size * head_dim), jnp.bfloat16),
+        in_specs=on_chip(3 + 2 * len(ways)),
+        out_specs=on_chip(1)[0],
         compiler_params=PARAMS,
         name="merge",
-    )(tag, own, own_log, *tags, *returned, *weights)
+    )(tag, own, own_log, *tags, *returned)
+    stack = pl.pallas_call(
+        copies_kernel,
+        out_shape=jax.ShapeDtypeStruct((lax.axis_size("x"), 2) + out_weight.shape, out_weight.dtype),
+        in_specs=[IN_HBM] * 2,
+        out_specs=IN_HBM,
+        scratch_shapes=[pltpu.VMEM(out_weight.shape, out_weight.dtype)] * 2
+        + [pltpu.SemaphoreType.DMA((2 * lax.axis_size("x"),))],
+        compiler_params=pltpu.CompilerParams(vmem_limit_bytes=62 * 1024 * 1024),
+        name="copies",
+    )(*weights)
     return project(attended, stack)
 
 

time: 136 us -> 127 us (0.934)
  the two profiles are of different devices: /device:TPU:163 before, /device:TPU:2 now
where the time goes in v3:
time: 127 us
  starting transfers between devices  69.6 us (55%)
  blocking collectives  22 us (17%)
  waiting for transfers between devices  19.7 us (16%)
  Pallas kernels  11.2 us (9%)
  local copies, waits for them, and re-layouts  2.31 us (2%)
  between operations  1.66 us (1%)
    ppermute x9, starting transfers between devices, swap(): return lax.ppermute(value, axis, [(i, i ^ bit) for i in range(count)])  38.1 us
    all_to_all x1, blocking collectives, project(): lax.all_to_all(terms.reshape((-1,) + block[3:]), ('zl', 'x', 'y'), 0, 0)  22 us
    ppermute x4, starting transfers between devices, body(): arrived = [lax.ppermute(packed, THREAD, way) for way in ways]  15.8 us
    ppermute x9, waiting for transfers between devices, swap(): return lax.ppermute(value, axis, [(i, i ^ bit) for i in range(count)])  13.6 us
    ppermute x4, starting transfers between devices, body(): lax.ppermute(part, THREAD, way)  9.79 us
    all_to_all x1, starting transfers between devices, project(): weights = lax.all_to_all(stack, 'x', 0, 0)  5.84 us
    all_to_all x1, waiting for transfers between devices, project(): weights = lax.all_to_all(stack, 'x', 0, 0)  5.76 us
    pallas_call x1, Pallas kernels, body(): pl.pallas_call(near_kernel, out_shape=[jax.ShapeDtypeStruct(packed.shape,...  4.17 us
  transfers between devices with their start and end apart: 18, of which 7 were waited for; matrix products, arithmetic and copies ran while one was open for 0% of the time, Pallas kernels for 4%

profile of v3, /device:TPU:2, one launch (start us, length us, event | category | flops | bytes accessed | tf_op | source)
XLA Modules:
  0.0 126.8 jit_solution(5890140679439088328)
XLA Ops:
  1.8 7.9 %collective-permute-start.1 = (bf16[528,128]{1,0:T(8,128)(2,1)S(1)}, bf16[528,128]{1,0:T(8,128)(2,1)S(1)}, u32[]{:S(2)}, u32[]{:S(2)}) collective-permute-start(bf16[528,128]{1,0:T(8,128)(2,1)S(1)} %get-tuple-element.14.query_ref), channel_id=1, source_target_pairs={{0,16},{16,0},{8,24},{24,8},{32,48},{48,32},{40,56},{56,40},{64,80... | collective-permute-start | bytes 405512 | tf_op jit(solution)/shard_map/ppermute | solution.py:283
  9.7 1.9 %collective-permute-start.2 = (bf16[528,128]{1,0:T(8,128)(2,1)S(1)}, bf16[528,128]{1,0:T(8,128)(2,1)S(1)}, u32[]{:S(2)}, u32[]{:S(2)}) collective-permute-start(bf16[528,128]{1,0:T(8,128)(2,1)S(1)} %get-tuple-element.14.query_ref), channel_id=1, source_target_pairs={{16,32},{32,16},{24,40},{40,24},{48,64},{64,48},{56,72},{72,56},{8... | collective-permute-start | bytes 405512 | tf_op jit(solution)/shard_map/ppermute | solution.py:283
  11.7 1.9 %collective-permute-start.3 = (bf16[528,128]{1,0:T(8,128)(2,1)S(1)}, bf16[528,128]{1,0:T(8,128)(2,1)S(1)}, u32[]{:S(2)}, u32[]{:S(2)}) collective-permute-start(bf16[528,128]{1,0:T(8,128)(2,1)S(1)} %get-tuple-element.14.query_ref), channel_id=1, source_target_pairs={{8,16},{16,8},{24,32},{32,24},{40,48},{48,40},{56,64},{64,56},{72,... | collective-permute-start | bytes 405512 | tf_op jit(solution)/shard_map/ppermute | solution.py:283
  13.6 4.0 %collective-permute-start.4 = (bf16[528,128]{1,0:T(8,128)(2,1)S(1)}, bf16[528,128]{1,0:T(8,128)(2,1)S(1)}, u32[]{:S(2)}, u32[]{:S(2)}) collective-permute-start(bf16[528,128]{1,0:T(8,128)(2,1)S(1)} %get-tuple-element.14.query_ref), channel_id=1, source_target_pairs={{0,8},{8,0},{16,24},{24,16},{32,40},{40,32},{48,56},{56,48},{64,72... | collective-permute-start | bytes 405512 | tf_op jit(solution)/shard_map/ppermute | solution.py:283
  18.6 4.2 %near.1 = (bf16[528,128]{1,0:T(8,128)(2,1)S(1)}, bf16[528,128]{1,0:T(8,128)(2,1)S(1)}, bf16[528,128]{1,0:T(8,128)(2,1)S(1)}, bf16[528,128]{1,0:T(8,128)(2,1)S(1)}) custom-call(s32[1]{0:T(128)S(6)} %copy.15.length_ref, bf16[16,128]{1,0:T(8,128)(2,1)S(1)} %get-tuple-element.13.own_tag_ref, bf16[2048,128]{1,0:T(8,128)(2,1)S(1)} %bitcast.27, ...), custom_call_target="tpu_custom_call" | custom-call | tf_op jit(solution)/shard_map/near/pallas_call | solution.py:297
  22.8 1.9 %collective-permute-start.5 = (bf16[528,128]{1,0:T(8,128)(2,1)S(1)}, bf16[528,128]{1,0:T(8,128)(2,1)S(1)}, u32[]{:S(2)}, u32[]{:S(2)}) collective-permute-start(bf16[528,128]{1,0:T(8,128)(2,1)S(1)} %get-tuple-element.17), channel_id=1, source_target_pairs={{0,16},{16,0},{8,24},{24,8},{32,48},{48,32},{40,56},{56,40},{64,80... | collective-permute-start | bytes 405512 | tf_op jit(solution)/shard_map/ppermute | solution.py:306
  24.7 1.9 %collective-permute-start.6 = (bf16[528,128]{1,0:T(8,128)(2,1)S(1)}, bf16[528,128]{1,0:T(8,128)(2,1)S(1)}, u32[]{:S(2)}, u32[]{:S(2)}) collective-permute-start(bf16[528,128]{1,0:T(8,128)(2,1)S(1)} %get-tuple-element.18), channel_id=1, source_target_pairs={{16,32},{32,16},{24,40},{40,24},{48,64},{64,48},{56,72},{72,56},{8... | collective-permute-start | bytes 405512 | tf_op jit(solution)/shard_map/ppermute | solution.py:306
  26.7 1.9 %collective-permute-start.7 = (bf16[528,128]{1,0:T(8,128)(2,1)S(1)}, bf16[528,128]{1,0:T(8,128)(2,1)S(1)}, u32[]{:S(2)}, u32[]{:S(2)}) collective-permute-start(bf16[528,128]{1,0:T(8,128)(2,1)S(1)} %get-tuple-element.19), channel_id=1, source_target_pairs={{8,16},{16,8},{24,32},{32,24},{40,48},{48,40},{56,64},{64,56},{72,... | collective-permute-start | bytes 405512 | tf_op jit(solution)/shard_map/ppermute | solution.py:306
  28.6 4.0 %collective-permute-start.8 = (bf16[528,128]{1,0:T(8,128)(2,1)S(1)}, bf16[528,128]{1,0:T(8,128)(2,1)S(1)}, u32[]{:S(2)}, u32[]{:S(2)}) collective-permute-start(bf16[528,128]{1,0:T(8,128)(2,1)S(1)} %get-tuple-element.20), channel_id=1, source_target_pairs={{0,8},{8,0},{16,24},{24,16},{32,40},{40,32},{48,56},{56,48},{64,72... | collective-permute-start | bytes 405512 | tf_op jit(solution)/shard_map/ppermute | solution.py:306
  32.6 3.3 %collective-permute-start = (bf16[1024,128]{1,0:T(8,128)(2,1)S(1)}, bf16[1024,128]{1,0:T(8,128)(2,1)S(1)}, u32[]{:S(2)}, u32[]{:S(2)}) collective-permute-start(bf16[1024,128]{1,0:T(8,128)(2,1)S(1)} %copy-done.5), channel_id=1, source_target_pairs={{0,64},{64,0},{1,65},{65,1},{2,66},{66,2},{3,67},{67,3},{4,68},{68... | collective-permute-start | bytes 786440 | tf_op jit(solution)/shard_map/ppermute | solution.py:225
  38.5 8.3 %collective-permute-start.12 = (bf16[64,1024]{1,0:T(8,128)(2,1)S(1)}, bf16[64,1024]{1,0:T(8,128)(2,1)S(1)}, u32[]{:S(2)}, u32[]{:S(2)}) collective-permute-start(bf16[64,1024]{1,0:T(8,128)(2,1)S(1)} %merge.1.refs_0_), channel_id=1, source_target_pairs={{0,256},{256,0},{1,257},{257,1},{2,258},{258,2},{3,259},{259,3},{4... | collective-permute-start | bytes 393224 | tf_op jit(solution)/shard_map/ppermute | solution.py:225
  47.6 2.4 %copies.1 = bf16[4,2,1024,128]{3,2,1,0:T(8,128)(2,1)} custom-call(bf16[1024,128]{1,0:T(8,128)(2,1)} %first_hbm.1, bf16[1024,128]{1,0:T(8,128)(2,1)} %copy-done.6), custom_call_target="tpu_custom_call" | custom-call | tf_op jit(solution)/shard_map/copies/pallas_call | solution.py:316
  50.0 5.8 %all-to-all-start = ((bf16[4,2,1024,128]{3,2,1,0:T(8,128)(2,1)}), bf16[4,2,1024,128]{3,2,1,0:T(8,128)(2,1)S(1)}, u32[]{:S(2)}, u32[]{:S(2)}) async-start(bf16[4,2,1024,128]{3,2,1,0:T(8,128)(2,1)} %copies.1), calls=%async_computation | async-start | bytes 4194304 | tf_op jit(solution)/shard_map/all_to_all | solution.py:232
  55.9 3.0 %collective-permute-start.10 = (bf16[64,1024]{1,0:T(8,128)(2,1)S(1)}, bf16[64,1024]{1,0:T(8,128)(2,1)S(1)}, u32[]{:S(2)}, u32[]{:S(2)}) collective-permute-start(bf16[64,1024]{1,0:T(8,128)(2,1)S(1)} %merge.1.refs_0_), channel_id=1, source_target_pairs={{0,128},{128,0},{1,129},{129,1},{2,130},{130,2},{3,131},{131,3},{4... | collective-permute-start | bytes 393224 | tf_op jit(solution)/shard_map/ppermute | solution.py:225
  59.5 3.2 %collective-permute-start.14 = (bf16[64,1024]{1,0:T(8,128)(2,1)S(1)}, bf16[64,1024]{1,0:T(8,128)(2,1)S(1)}, u32[]{:S(2)}, u32[]{:S(2)}) collective-permute-start(bf16[64,1024]{1,0:T(8,128)(2,1)S(1)} %relay.1.refs_4_), channel_id=1, source_target_pairs={{0,128},{128,0},{1,129},{129,1},{2,130},{130,2},{3,131},{131,3},{4... | collective-permute-start | bytes 393224 | tf_op jit(solution)/shard_map/ppermute | solution.py:225
  62.7 1.9 %collective-permute-start.9 = (bf16[64,1024]{1,0:T(8,128)(2,1)S(1)}, bf16[64,1024]{1,0:T(8,128)(2,1)S(1)}, u32[]{:S(2)}, u32[]{:S(2)}) collective-permute-start(bf16[64,1024]{1,0:T(8,128)(2,1)S(1)} %merge.1.refs_0_), channel_id=1, source_target_pairs={{0,8},{8,0},{1,9},{9,1},{2,10},{10,2},{3,11},{11,3},{4,12},{12,4},... | collective-permute-start | bytes 393224 | tf_op jit(solution)/shard_map/ppermute | solution.py:225
  64.6 2.4 %collective-permute-start.13 = (bf16[64,1024]{1,0:T(8,128)(2,1)S(1)}, bf16[64,1024]{1,0:T(8,128)(2,1)S(1)}, u32[]{:S(2)}, u32[]{:S(2)}) collective-permute-start(bf16[64,1024]{1,0:T(8,128)(2,1)S(1)} %relay.1.refs_4_), channel_id=1, source_target_pairs={{0,8},{8,0},{1,9},{9,1},{2,10},{10,2},{3,11},{11,3},{4,12},{12,4},... | collective-permute-start | bytes 393224 | tf_op jit(solution)/shard_map/ppermute | solution.py:225
  67.0 2.3 %collective-permute-done.10.refs_2_ = bf16[64,1024]{1,0:T(8,128)(2,1)S(1)} collective-permute-done((bf16[64,1024]{1,0:T(8,128)(2,1)S(1)}, bf16[64,1024]{1,0:T(8,128)(2,1)S(1)}, u32[]{:S(2)}, u32[]{:S(2)}) %collective-permute-start.10) | collective-permute-done | bytes 131104 | tf_op jit(solution)/shard_map/ppermute | solution.py:225
  71.4 2.3 %collective-permute-start.15 = (bf16[64,1024]{1,0:T(8,128)(2,1)S(1)}, bf16[64,1024]{1,0:T(8,128)(2,1)S(1)}, u32[]{:S(2)}, u32[]{:S(2)}) collective-permute-start(bf16[64,1024]{1,0:T(8,128)(2,1)S(1)} %collective-permute-done.14.refs_6_), channel_id=1, source_target_pairs={{0,8},{8,0},{1,9},{9,1},{2,10},{10,2},{3,11},{11,3},{4,12},{12,4},... | collective-permute-start | bytes 393224 | tf_op jit(solution)/shard_map/ppermute | solution.py:225
  74.6 5.8 %all-to-all-done.weight_ref = bf16[4,2,1024,128]{3,2,1,0:T(8,128)(2,1)S(1)} async-done(((bf16[4,2,1024,128]{3,2,1,0:T(8,128)(2,1)}), bf16[4,2,1024,128]{3,2,1,0:T(8,128)(2,1)S(1)}, u32[]{:S(2)}, u32[]{:S(2)}) %all-to-all-start) | async-done | bytes 2097184 | tf_op jit(solution)/shard_map/all_to_all | solution.py:232
  80.4 1.9 %project.1 = bf16[2,4,4,2,64,128]{5,4,3,2,1,0:T(8,128)(2,1)S(1)} custom-call(s32[3]{0:T(128)S(1)} %pad_add_fusion.place_ref, bf16[4,2,1024,128]{3,2,1,0:T(8,128)(2,1)S(1)} %all-to-all-done.weight_ref, bf16[64,1024]{1,0:T(8,128)(2,1)S(1)} %merge.1.refs_0_, bf16[64,1024]{1,0:T(8,128)(2,1)S(1)} %collective-permute-done.9.refs_1_, ...), custom_call_target="tpu_custom_call" | custom-call | tf_op jit(solution)/shard_map/project/pallas_call | solution.py:248
  82.3 22.0 %all_to_all.10 = bf16[32,2,64,128]{3,2,1,0:T(8,128)(2,1)S(1)} all-to-all(bf16[32,2,64,128]{3,2,1,0:T(8,128)(2,1)S(1)} %bitcast.26), channel_id=1, replica_groups=mesh['zt'=2,'zm'=2,'zl'=2,'x'=4,'c'=2,'w'=2,'y'=4] {'zl','x','y'}, dimensions={0} | all-to-all | bytes 2097152 | tf_op jit(solution)/shard_map/all_to_all | solution.py:257
  104.5 11.8 %collective-permute-start.16 = (bf16[2,4,64,128]{3,2,1,0:T(8,128)(2,1)S(1)}, bf16[2,4,64,128]{3,2,1,0:T(8,128)(2,1)S(1)}, u32[]{:S(2)}, u32[]{:S(2)}) collective-permute-start(bf16[2,4,64,128]{3,2,1,0:T(8,128)(2,1)S(1)} %fusion.2), channel_id=1, source_target_pairs={{0,68},{4,64},{64,4},{68,0},{1,69},{5,65},{65,5},{69,1},{2,70},{6,... | collective-permute-start | bytes 393224 | tf_op jit(solution)/shard_map/ppermute | solution.py:225
  116.3 9.7 %collective-permute-done.16 = bf16[2,4,64,128]{3,2,1,0:T(8,128)(2,1)S(1)} collective-permute-done((bf16[2,4,64,128]{3,2,1,0:T(8,128)(2,1)S(1)}, bf16[2,4,64,128]{3,2,1,0:T(8,128)(2,1)S(1)}, u32[]{:S(2)}, u32[]{:S(2)}) %collective-permute-start.16) | collective-permute-done | bytes 131104 | tf_op jit(solution)/shard_map/ppermute | solution.py:225
  (43 shorter events, 9.2 us)
Async XLA Ops:
  0.7 0.9 copy-start.4
  1.6 17.1 %copy-start = (bf16[1,2048,1,128]{3,1,2,0:T(8,128)(2,1)S(1)}, bf16[1,2048,1,128]{3,1,2,0:T(8,128)(2,1)}, u32[]{:S(2)}) copy-start(bf16[1,2048,1,128]{3,1,2,0:T(8,128)(2,1)} %param.13) | copy-start | bytes 1572868
  1.6 17.1 %copy-start.1 = (bf16[1,2048,1,128]{3,1,2,0:T(8,128)(2,1)S(1)}, bf16[1,2048,1,128]{3,1,2,0:T(8,128)(2,1)}, u32[]{:S(2)}) copy-start(bf16[1,2048,1,128]{3,1,2,0:T(8,128)(2,1)} %param.14) | copy-start | bytes 1572868
  1.6 17.1 %copy-start.2 = (bf16[1,64,1,128]{3,1,2,0:T(8,128)(2,1)S(1)}, bf16[1,64,1,128]{3,1,2,0:T(8,128)(2,1)}, u32[]{:S(2)}) copy-start(bf16[1,64,1,128]{3,1,2,0:T(8,128)(2,1)} %param.11) | copy-start | bytes 49156
  1.6 17.1 %copy-start.3 = (bf16[1,64,1,128]{3,1,2,0:T(8,128)(2,1)S(1)}, bf16[1,64,1,128]{3,1,2,0:T(8,128)(2,1)}, u32[]{:S(2)}) copy-start(bf16[1,64,1,128]{3,1,2,0:T(8,128)(2,1)} %param.12) | copy-start | bytes 49156
  1.6 31.0 %copy-start.5 = (bf16[1024,128]{1,0:T(8,128)(2,1)S(1)}, bf16[1024,128]{1,0:T(8,128)(2,1)}, u32[]{:S(2)}) copy-start(bf16[1024,128]{1,0:T(8,128)(2,1)} %first_hbm.1) | copy-start | bytes 786436
  1.8 16.5 %collective-permute-start.1 = (bf16[528,128]{1,0:T(8,128)(2,1)S(1)}, bf16[528,128]{1,0:T(8,128)(2,1)S(1)}, u32[]{:S(2)}, u32[]{:S(2)}) collective-permute-start(bf16[528,128]{1,0:T(8,128)(2,1)S(1)} %get-tuple-element.14.query_ref), channel_id=1, source_target_pairs={{0,16},{16,0},{8,24},{24,8},{32,48},{48,32},{40,56},{56,40},{64,80... | collective-permute-start | bytes 405512 | tf_op jit(solution)/shard_map/ppermute | solution.py:283
  9.7 8.6 %collective-permute-start.2 = (bf16[528,128]{1,0:T(8,128)(2,1)S(1)}, bf16[528,128]{1,0:T(8,128)(2,1)S(1)}, u32[]{:S(2)}, u32[]{:S(2)}) collective-permute-start(bf16[528,128]{1,0:T(8,128)(2,1)S(1)} %get-tuple-element.14.query_ref), channel_id=1, source_target_pairs={{16,32},{32,16},{24,40},{40,24},{48,64},{64,48},{56,72},{72,56},{8... | collective-permute-start | bytes 405512 | tf_op jit(solution)/shard_map/ppermute | solution.py:283
  11.7 6.6 %collective-permute-start.3 = (bf16[528,128]{1,0:T(8,128)(2,1)S(1)}, bf16[528,128]{1,0:T(8,128)(2,1)S(1)}, u32[]{:S(2)}, u32[]{:S(2)}) collective-permute-start(bf16[528,128]{1,0:T(8,128)(2,1)S(1)} %get-tuple-element.14.query_ref), channel_id=1, source_target_pairs={{8,16},{16,8},{24,32},{32,24},{40,48},{48,40},{56,64},{64,56},{72,... | collective-permute-start | bytes 405512 | tf_op jit(solution)/shard_map/ppermute | solution.py:283
  13.6 5.0 %collective-permute-start.4 = (bf16[528,128]{1,0:T(8,128)(2,1)S(1)}, bf16[528,128]{1,0:T(8,128)(2,1)S(1)}, u32[]{:S(2)}, u32[]{:S(2)}) collective-permute-start(bf16[528,128]{1,0:T(8,128)(2,1)S(1)} %get-tuple-element.14.query_ref), channel_id=1, source_target_pairs={{0,8},{8,0},{16,24},{24,16},{32,40},{40,32},{48,56},{56,48},{64,72... | collective-permute-start | bytes 405512 | tf_op jit(solution)/shard_map/ppermute | solution.py:283
  22.8 15.1 %collective-permute-start.5 = (bf16[528,128]{1,0:T(8,128)(2,1)S(1)}, bf16[528,128]{1,0:T(8,128)(2,1)S(1)}, u32[]{:S(2)}, u32[]{:S(2)}) collective-permute-start(bf16[528,128]{1,0:T(8,128)(2,1)S(1)} %get-tuple-element.17), channel_id=1, source_target_pairs={{0,16},{16,0},{8,24},{24,8},{32,48},{48,32},{40,56},{56,40},{64,80... | collective-permute-start | bytes 405512 | tf_op jit(solution)/shard_map/ppermute | solution.py:306
  24.7 13.2 %collective-permute-start.6 = (bf16[528,128]{1,0:T(8,128)(2,1)S(1)}, bf16[528,128]{1,0:T(8,128)(2,1)S(1)}, u32[]{:S(2)}, u32[]{:S(2)}) collective-permute-start(bf16[528,128]{1,0:T(8,128)(2,1)S(1)} %get-tuple-element.18), channel_id=1, source_target_pairs={{16,32},{32,16},{24,40},{40,24},{48,64},{64,48},{56,72},{72,56},{8... | collective-permute-start | bytes 405512 | tf_op jit(solution)/shard_map/ppermute | solution.py:306
  26.7 11.3 %collective-permute-start.7 = (bf16[528,128]{1,0:T(8,128)(2,1)S(1)}, bf16[528,128]{1,0:T(8,128)(2,1)S(1)}, u32[]{:S(2)}, u32[]{:S(2)}) collective-permute-start(bf16[528,128]{1,0:T(8,128)(2,1)S(1)} %get-tuple-element.19), channel_id=1, source_target_pairs={{8,16},{16,8},{24,32},{32,24},{40,48},{48,40},{56,64},{64,56},{72,... | collective-permute-start | bytes 405512 | tf_op jit(solution)/shard_map/ppermute | solution.py:306
  28.6 9.3 %collective-permute-start.8 = (bf16[528,128]{1,0:T(8,128)(2,1)S(1)}, bf16[528,128]{1,0:T(8,128)(2,1)S(1)}, u32[]{:S(2)}, u32[]{:S(2)}) collective-permute-start(bf16[528,128]{1,0:T(8,128)(2,1)S(1)} %get-tuple-element.20), channel_id=1, source_target_pairs={{0,8},{8,0},{16,24},{24,16},{32,40},{40,32},{48,56},{56,48},{64,72... | collective-permute-start | bytes 405512 | tf_op jit(solution)/shard_map/ppermute | solution.py:306
  32.6 14.3 %collective-permute-start = (bf16[1024,128]{1,0:T(8,128)(2,1)S(1)}, bf16[1024,128]{1,0:T(8,128)(2,1)S(1)}, u32[]{:S(2)}, u32[]{:S(2)}) collective-permute-start(bf16[1024,128]{1,0:T(8,128)(2,1)S(1)} %copy-done.5), channel_id=1, source_target_pairs={{0,64},{64,0},{1,65},{65,1},{2,66},{66,2},{3,67},{67,3},{4,68},{68... | collective-permute-start | bytes 786440 | tf_op jit(solution)/shard_map/ppermute | solution.py:225
  38.5 20.9 %collective-permute-start.12 = (bf16[64,1024]{1,0:T(8,128)(2,1)S(1)}, bf16[64,1024]{1,0:T(8,128)(2,1)S(1)}, u32[]{:S(2)}, u32[]{:S(2)}) collective-permute-start(bf16[64,1024]{1,0:T(8,128)(2,1)S(1)} %merge.1.refs_0_), channel_id=1, source_target_pairs={{0,256},{256,0},{1,257},{257,1},{2,258},{258,2},{3,259},{259,3},{4... | collective-permute-start | bytes 393224 | tf_op jit(solution)/shard_map/ppermute | solution.py:225
  50.0 30.3 %all-to-all-start = ((bf16[4,2,1024,128]{3,2,1,0:T(8,128)(2,1)}), bf16[4,2,1024,128]{3,2,1,0:T(8,128)(2,1)S(1)}, u32[]{:S(2)}, u32[]{:S(2)}) async-start(bf16[4,2,1024,128]{3,2,1,0:T(8,128)(2,1)} %copies.1), calls=%async_computation | async-start | bytes 4194304 | tf_op jit(solution)/shard_map/all_to_all | solution.py:232
  55.9 13.4 %collective-permute-start.10 = (bf16[64,1024]{1,0:T(8,128)(2,1)S(1)}, bf16[64,1024]{1,0:T(8,128)(2,1)S(1)}, u32[]{:S(2)}, u32[]{:S(2)}) collective-permute-start(bf16[64,1024]{1,0:T(8,128)(2,1)S(1)} %merge.1.refs_0_), channel_id=1, source_target_pairs={{0,128},{128,0},{1,129},{129,1},{2,130},{130,2},{3,131},{131,3},{4... | collective-permute-start | bytes 393224 | tf_op jit(solution)/shard_map/ppermute | solution.py:225
  59.5 11.9 %collective-permute-start.14 = (bf16[64,1024]{1,0:T(8,128)(2,1)S(1)}, bf16[64,1024]{1,0:T(8,128)(2,1)S(1)}, u32[]{:S(2)}, u32[]{:S(2)}) collective-permute-start(bf16[64,1024]{1,0:T(8,128)(2,1)S(1)} %relay.1.refs_4_), channel_id=1, source_target_pairs={{0,128},{128,0},{1,129},{129,1},{2,130},{130,2},{3,131},{131,3},{4... | collective-permute-start | bytes 393224 | tf_op jit(solution)/shard_map/ppermute | solution.py:225
  62.7 11.1 %collective-permute-start.9 = (bf16[64,1024]{1,0:T(8,128)(2,1)S(1)}, bf16[64,1024]{1,0:T(8,128)(2,1)S(1)}, u32[]{:S(2)}, u32[]{:S(2)}) collective-permute-start(bf16[64,1024]{1,0:T(8,128)(2,1)S(1)} %merge.1.refs_0_), channel_id=1, source_target_pairs={{0,8},{8,0},{1,9},{9,1},{2,10},{10,2},{3,11},{11,3},{4,12},{12,4},... | collective-permute-start | bytes 393224 | tf_op jit(solution)/shard_map/ppermute | solution.py:225
  64.6 9.2 %collective-permute-start.13 = (bf16[64,1024]{1,0:T(8,128)(2,1)S(1)}, bf16[64,1024]{1,0:T(8,128)(2,1)S(1)}, u32[]{:S(2)}, u32[]{:S(2)}) collective-permute-start(bf16[64,1024]{1,0:T(8,128)(2,1)S(1)} %relay.1.refs_4_), channel_id=1, source_target_pairs={{0,8},{8,0},{1,9},{9,1},{2,10},{10,2},{3,11},{11,3},{4,12},{12,4},... | collective-permute-start | bytes 393224 | tf_op jit(solution)/shard_map/ppermute | solution.py:225
  69.3 4.4 %collective-permute-start.11 = (bf16[64,1024]{1,0:T(8,128)(2,1)S(1)}, bf16[64,1024]{1,0:T(8,128)(2,1)S(1)}, u32[]{:S(2)}, u32[]{:S(2)}) collective-permute-start(bf16[64,1024]{1,0:T(8,128)(2,1)S(1)} %collective-permute-done.10.refs_2_), channel_id=1, source_target_pairs={{0,8},{8,0},{1,9},{9,1},{2,10},{10,2},{3,11},{11,3},{4,12},{12,4},... | collective-permute-start | bytes 393224 | tf_op jit(solution)/shard_map/ppermute | solution.py:225
  71.4 3.2 %collective-permute-start.15 = (bf16[64,1024]{1,0:T(8,128)(2,1)S(1)}, bf16[64,1024]{1,0:T(8,128)(2,1)S(1)}, u32[]{:S(2)}, u32[]{:S(2)}) collective-permute-start(bf16[64,1024]{1,0:T(8,128)(2,1)S(1)} %collective-permute-done.14.refs_6_), channel_id=1, source_target_pairs={{0,8},{8,0},{1,9},{9,1},{2,10},{10,2},{3,11},{11,3},{4,12},{12,4},... | collective-permute-start | bytes 393224 | tf_op jit(solution)/shard_map/ppermute | solution.py:225
  104.5 21.5 %collective-permute-start.16 = (bf16[2,4,64,128]{3,2,1,0:T(8,128)(2,1)S(1)}, bf16[2,4,64,128]{3,2,1,0:T(8,128)(2,1)S(1)}, u32[]{:S(2)}, u32[]{:S(2)}) collective-permute-start(bf16[2,4,64,128]{3,2,1,0:T(8,128)(2,1)S(1)} %fusion.2), channel_id=1, source_target_pairs={{0,68},{4,64},{64,4},{68,0},{1,69},{5,65},{65,5},{69,1},{2,70},{6,... | collective-permute-start | bytes 393224 | tf_op jit(solution)/shard_map/ppermute | solution.py:225
  (1 other events, 0.7 us)
